TPU v7x, 256 devices: a whole 4x4x8 slice. The times are simulated.
256 devices in a mesh: step: 4 (over x), node: 64 (over z, y, core).
Axes of the slice: x: 4, y: 4, z: 8, core: 2. Of those that a mesh axis runs over, the one named last changes fastest.
Arguments:
- states: bfloat16 [4, 16384, 512], P('step', 'node'), may hold values from -16 to 16
- step_cotangents: float32 [4, 16384, 512], P('step', 'node'), may hold values from -6 to 6
- weights: bfloat16 [512, 3072], replicated, may hold values from -0.25 to 0.25
- edge_tiles: bfloat16 [64, 16, 128, 128], P('node'), may hold values from -0.1875 to 0.1875
- tile_src: int32 [64, 16], P('node'), may hold values from 0 to 5, as said below
- tile_dst: int32 [64, 16], P('node'), may hold values from 0 to 1
- tile_counts: int32 [64], P('node'), may hold values from 4 to 16, as said below
Outputs:
- state_adjoints: float32 [4, 16384, 512], P('step', 'node')
- weight_grads: float32 [512, 3072], P('node')
Inputs may be any that keep to these rules, and one draw needn't show every extreme that they name: `tile_src`: slot 0 of every device names a block below 2 and slot 1 one from 4. `tile_counts`: some device has all 16 slots live.
All inputs are finite; a program needn't handle non-finite values.
Results may differ from a plain program's by a relative error of at most 0.029.
Values may be sent and summed in bfloat16 or wider, within the bound.
No kernel may reach another device: no remote copies, remote signals or barrier semaphores. Data moves between devices by JAX's collectives and lax.ppermute only.
A program may use at most 128 MiB of HBM per device.

v0:
```python
import math

import jax
import jax.numpy as jnp
from jax import lax
from jax.sharding import PartitionSpec as P

Z, Y, C = 8, 4, 2
NODES = Z * Y * C
STEPS = 4
SPLIT = 2
F32 = jnp.float32
BF16 = jnp.bfloat16


def place(z, y, c):
    return (z * Y + y) * C + c


def split(p):
    return p // (Y * C), (p // C) % Y, p % C


def snake(p):
    z, y, c = split(p)
    return place(z, y if z % 2 == 0 else Y - 1 - y, c)


def beyond(q):
    return (q + 1) % NODES if q % 2 else (q - 1) % NODES


DEVICES = range(NODES)
FLIP = [(snake(p), p) for p in DEVICES]
OUTER = [(p, snake(beyond(snake(p)))) for p in DEVICES]
OUTER_HOME = [(beyond(snake(p)), p) for p in DEVICES]
SIBLING = [(p, p ^ 1) for p in DEVICES]
Z_GROUPS = [[place(z, y, c) for z in range(Z)] for y in range(Y) for c in range(C)]


def over_node(value, pairs):
    return lax.ppermute(value, "node", pairs)


def over_step(value, k):
    return lax.ppermute(value, "step", [(s, s ^ k) for s in range(STEPS)])


def over_both(value, k):
    pairs = [((s ^ k) * NODES + snake(p), s * NODES + p) for s in range(STEPS) for p in DEVICES]
    return lax.ppermute(value, ("step", "node"), pairs)


def y_pairs(k):
    return [(place(z, y, c), place(z, y ^ k, c)) for z in range(Z) for y in range(Y) for c in range(C)]


def mul(left, right):
    return jnp.dot(left, right, preferred_element_type=F32)


def mul_t(left, right):
    return lax.dot_general(left, right, (((1,), (1,)), ((), ())), preferred_element_type=F32)


def t_mul(left, right):
    return lax.dot_general(left, right, (((0,), (0,)), ((), ())), preferred_element_type=F32)


def assemble(tiles, sources, targets, count, core, nblk):
    slots, block = tiles.shape[0], tiles.shape[1]
    third = sources // nblk
    third = jnp.where(core == 1, 2 - third, third)
    column = third * nblk + sources % nblk
    cell = targets * (3 * nblk) + column
    live = jnp.arange(slots) < count
    hot = ((cell[None, :] == jnp.arange(3 * nblk * nblk)[:, None]) & live[None, :]).astype(BF16)
    blocks = lax.dot_general(hot, tiles, (((1,), (0,)), ((), ())), preferred_element_type=F32)
    blocks = blocks.astype(BF16).reshape(nblk, 3 * nblk, block, block)
    return blocks.transpose(0, 2, 1, 3).reshape(nblk * block, 3 * nblk * block)


def feature_choice(width, x, yi, ci, per):
    column = lax.broadcasted_iota(jnp.int32, (1, width), 1)
    row = lax.broadcasted_iota(jnp.int32, (width, 1), 0)
    row_of = column % per
    rest = column // per
    z, rest = rest % Z, rest // Z
    y, rest = rest % Y, rest // Y
    c, k = rest % C, rest // C
    feature = place(z, y ^ yi, c ^ ci) * (per * SPLIT) + ((x & 1) ^ k) * per + row_of
    return (row == feature).astype(BF16)


def after(value, *others):
    return lax.optimization_barrier((value, *others))[0]


def on_device(states, step_cotangents, weights, edge_tiles, tile_src, tile_dst, tile_counts):
    rows, width = states.shape[1], states.shape[2]
    layers = weights.shape[1] // (3 * width)
    nblk = rows // edge_tiles.shape[2]
    me = lax.axis_index("node")
    x = lax.axis_index("step")
    zi, yi, ci = split(me)
    w = [
        [weights[:, (3 * layer + j) * width : (3 * layer + j + 1) * width] for j in range(3)]
        for layer in range(layers)
    ]

    hb = over_node(states[0], FLIP)
    outer = over_node(states[0], OUTER_HOME)
    matrix = assemble(edge_tiles[0], tile_src[0], tile_dst[0], tile_counts[0], ci, nblk)
    cot = after(step_cotangents[0], matrix).astype(BF16)
    matrix = over_node(matrix, FLIP)
    m_out, m_own, m_sib = (matrix[:, j * rows : (j + 1) * rows] for j in range(3))
    cot = over_node(cot, FLIP)

    h = hb.astype(F32)
    left_hand, slopes = [], []
    for layer in range(layers):
        wa, wb, wc = w[layer]
        if layer:
            hb = h.astype(BF16)
            outer = over_node(hb, OUTER)
        sib = over_node(hb, SIBLING)
        local = mul(m_own, hb)
        first = mul(hb, wa)
        mb = (local + mul(m_sib, sib) + mul(m_out, outer)).astype(BF16)
        zz = first + mul(mb, wb)
        sig = jax.nn.sigmoid(zz)
        g = (zz * sig).astype(BF16)
        slope = (sig * (1.0 + zz * (1.0 - sig))).astype(BF16)
        if layer + 1 < layers:
            h = h + mul(g, wc)
            slope = after(slope, h)
        slopes.append((slope, over_step(slope, 1)))
        left_hand += [hb, mb, g]
    cot = after(cot, left_hand[3])
    cots = (cot, over_step(cot, 1))
    n_out = over_node(m_out, OUTER)
    n_chip = jnp.concatenate([m_own, over_node(m_sib, SIBLING)], axis=0)

    own_first = (x & 1) == 1

    def of_turn(pair, turn):
        own, other = pair
        return jnp.where(own_first, other, own) if turn % 2 else jnp.where(own_first, own, other)

    upper = x >= 2
    share = width // SPLIT
    choice = feature_choice(width, x, yi, ci, width // NODES // SPLIT)
    crossing = {(1, 0): [3, 4, 5, 0], (2, 0): [1, 2]}

    def sum_rows(layer):
        pairs = [
            [jnp.where(upper, e, v) for e, v in zip(kept[turn - 2, layer], kept[turn, layer])]
            for turn in (2, 3)
        ]
        ab, dzb = [jnp.concatenate(v, axis=0) for v in zip(*pairs)]
        left = [
            jnp.concatenate([of_turn(v, turn) for turn in (2, 3)], axis=0)
            for v in lhs[3 * layer : 3 * layer + 3]
        ]
        return t_mul(jnp.concatenate(left[:2], axis=1), dzb), t_mul(left[2], ab)

    adjoint = None
    result = jnp.zeros((rows, width), F32)
    grads = [None] * layers
    kept, moving = {}, []
    for turn in range(STEPS):
        cot = of_turn(cots, turn).astype(F32)
        if turn == 0:
            adjoint = cot
        elif turn == 2:
            adjoint = cot + over_step(adjoint.astype(BF16), 3).astype(F32)
        else:
            adjoint = adjoint + cot
        for layer in range(layers - 1, -1, -1):
            wa, wb, wc = w[layer]
            ab = adjoint.astype(BF16)
            dzb = (mul_t(ab, wc) * of_turn(slopes[layer], turn).astype(F32)).astype(BF16)
            dm = mul_t(dzb, wb).astype(BF16)
            kept[turn, layer] = (ab, dzb)
            if moving:
                dm, got = lax.optimization_barrier((dm, tuple(lhs[k][1] for k in moving)))
                for k, v in zip(moving, got):
                    lhs[k][1] = v
                moving = []
            if turn == STEPS - 1 and layer == 0:
                keep, sent = split_cores(sum_rows(layer))
                grads[0] = keep + over_node(sent, SIBLING).astype(F32)
                dm = after(dm, sent)
            d_out = over_node(dm, OUTER)
            adjoint = adjoint + mul_t(dzb, wa)
            d_sib = over_node(after(dm, adjoint), SIBLING)
            if turn == 0 and layer == layers - 1:
                ordered = mul(jnp.concatenate(after(tuple(left_hand), dm), axis=0), choice).astype(BF16)
                ordered = ordered.reshape(len(left_hand), rows, width)
                lhs = [[v[:, :share], v[:, share:]] for v in ordered]
            if (turn, layer) in crossing:
                moving = crossing[turn, layer]
                joined = jnp.concatenate([after(lhs[k][1], dm) for k in moving], axis=1)
                joined = over_step(joined, 1)
                for j, k in enumerate(moving):
                    lhs[k][1] = joined[:, j * share : (j + 1) * share]
            if turn == STEPS - 1 and layer:
                kept[turn, layer] = after((ab, dzb), dm)
                keep, sent = split_cores(sum_rows(layer))
                grads[layer] = keep + over_node(sent, SIBLING).astype(F32)
            adjoint = adjoint + t_mul(n_chip, jnp.concatenate([dm, d_sib], axis=0)) + t_mul(n_out, d_out)
        result = jnp.where(x == STEPS - 1 - turn, adjoint, result)
    result = over_node(result.astype(BF16), FLIP).astype(F32)

    grad = jnp.concatenate(grads, axis=1)
    grad_b = grad.astype(BF16)
    chunk = grad.shape[0] // Y
    total = grad[:chunk]
    for k in (2, 1, 3):
        total = total + over_node(grad_b[k * chunk : (k + 1) * chunk], y_pairs(k)).astype(F32)
    sent = total.astype(BF16).reshape(Z, chunk // Z, -1)
    got = lax.all_to_all(sent, "node", 0, 0, axis_index_groups=Z_GROUPS, tiled=False)
    mine = jnp.sum(got.astype(F32), axis=0).astype(BF16)
    beside, same, across = [over_step(mine, k).astype(F32) for k in (1, 2, 3)]
    mine, beside = mine.astype(F32) + same, beside + across
    low = jnp.where(own_first, beside, mine)
    high = jnp.where(own_first, mine, beside)
    scale = 1.0 / math.sqrt(STEPS * rows * NODES)
    return (result[None], jnp.concatenate([low, high], axis=0) * scale)


def split_cores(sums):
    both, last = sums
    share = last.shape[0]
    half = share // C
    parts = [both[:share], both[share:], last]
    keep = jnp.concatenate([v[:half] for v in parts], axis=1)
    return keep, jnp.concatenate([v[half:] for v in parts], axis=1).astype(BF16)


def solution(mesh):
    return jax.shard_map(
        on_device,
        mesh=mesh,
        in_specs=(
            P("step", "node", None),
            P("step", "node", None),
            P(),
            P("node", None, None, None),
            P("node", None),
            P("node", None),
            P("node"),
        ),
        out_specs=(P("step", "node", None), P("node", None)),
        check_vma=False,
    )
```

profile of v0, /device:TPU:6, one launch (start us, length us, event | category | flops | bytes accessed | tf_op | source)
XLA Modules:
  0.0 164.6 jit_solution(12222020802958755399)
XLA Ops:
  4.8 10.6 %collective-permute-start.4 = (bf16[256,512]{1,0:T(8,128)(2,1)S(1)}, bf16[256,512]{1,0:T(8,128)(2,1)S(1)}, u32[]{:S(2)}, u32[]{:S(2)}) collective-permute-start(bf16[256,512]{1,0:T(8,128)(2,1)S(1)} %bitcast.75), channel_id=1, source_target_pairs={{63,0},{2,1},{1,2},{4,3},{3,4},{6,5},{5,6},{8,7},{13,8},{16,9},{11... | collective-permute-start | bytes 786440 | tf_op jit(solution)/shard_map/ppermute | solution.py:42
  15.4 1.4 collective-permute-start
  17.1 4.8 %collective-permute-done.4 = bf16[256,512]{1,0:T(8,128)(2,1)S(1)} collective-permute-done((bf16[256,512]{1,0:T(8,128)(2,1)S(1)}, bf16[256,512]{1,0:T(8,128)(2,1)S(1)}, u32[]{:S(2)}, u32[]{:S(2)}) %collective-permute-start.4) | collective-permute-done | bytes 262176 | tf_op jit(solution)/shard_map/ppermute | solution.py:42
  23.8 12.4 %collective-permute-start.7 = (bf16[256,512]{1,0:T(8,128)(2,1)S(1)}, bf16[256,512]{1,0:T(8,128)(2,1)S(1)}, u32[]{:S(2)}, u32[]{:S(2)}) collective-permute-start(bf16[256,512]{1,0:T(8,128)(2,1)S(1)} %convert_add_fusion.3), channel_id=1, source_target_pairs={{0,57},{1,2},{2,1},{3,4},{4,3},{5,6},{6,5},{7,14},{8,11},{9,16},{1... | collective-permute-start | bytes 786440 | tf_op jit(solution)/shard_map/ppermute | solution.py:42
  37.4 2.8 %collective-permute-done.7 = bf16[256,512]{1,0:T(8,128)(2,1)S(1)} collective-permute-done((bf16[256,512]{1,0:T(8,128)(2,1)S(1)}, bf16[256,512]{1,0:T(8,128)(2,1)S(1)}, u32[]{:S(2)}, u32[]{:S(2)}) %collective-permute-start.7) | collective-permute-done | bytes 262176 | tf_op jit(solution)/shard_map/ppermute | solution.py:42
  42.5 2.8 %collective-permute-start.11 = (bf16[256,256]{0,1:T(8,128)(2,1)S(1)}, bf16[256,256]{0,1:T(8,128)(2,1)S(1)}, u32[]{:S(2)}, u32[]{:S(2)}) collective-permute-start(bf16[256,256]{0,1:T(8,128)(2,1)S(1)} %get-tuple-element.118), channel_id=1, source_target_pairs={{0,57},{1,2},{2,1},{3,4},{4,3},{5,6},{6,5},{7,14},{8,11},{9,16},{1... | collective-permute-start | bytes 393224 | tf_op jit(solution)/shard_map/ppermute | solution.py:42
  49.1 4.9 %collective-permute-start.12 = (bf16[256,512]{1,0:T(8,128)(2,1)S(1)}, bf16[256,512]{1,0:T(8,128)(2,1)S(1)}, u32[]{:S(2)}, u32[]{:S(2)}) collective-permute-start(bf16[256,512]{1,0:T(8,128)(2,1)S(1)} %convolution_convert_fusion.9), channel_id=1, source_target_pairs={{0,57},{1,2},{2,1},{3,4},{4,3},{5,6},{6,5},{7,14},{8,11},{9,16},{1... | collective-permute-start | bytes 786440 | tf_op jit(solution)/shard_map/ppermute | solution.py:42
  54.2 3.8 %collective-permute-done.12 = bf16[256,512]{1,0:T(8,128)(2,1)S(1)} collective-permute-done((bf16[256,512]{1,0:T(8,128)(2,1)S(1)}, bf16[256,512]{1,0:T(8,128)(2,1)S(1)}, u32[]{:S(2)}, u32[]{:S(2)}) %collective-permute-start.12) | collective-permute-done | bytes 262176 | tf_op jit(solution)/shard_map/ppermute | solution.py:42
  59.3 3.0 %collective-permute-start.15 = (bf16[256,512]{1,0:T(8,128)(2,1)S(1)}, bf16[256,512]{1,0:T(8,128)(2,1)S(1)}, u32[]{:S(2)}, u32[]{:S(2)}) collective-permute-start(bf16[256,512]{1,0:T(8,128)(2,1)S(1)} %convolution_convert_fusion.8), channel_id=1, source_target_pairs={{0,57},{1,2},{2,1},{3,4},{4,3},{5,6},{6,5},{7,14},{8,11},{9,16},{1... | collective-permute-start | bytes 786440 | tf_op jit(solution)/shard_map/ppermute | solution.py:42
  63.0 3.4 %collective-permute-done.15 = bf16[256,512]{1,0:T(8,128)(2,1)S(1)} collective-permute-done((bf16[256,512]{1,0:T(8,128)(2,1)S(1)}, bf16[256,512]{1,0:T(8,128)(2,1)S(1)}, u32[]{:S(2)}, u32[]{:S(2)}) %collective-permute-start.15) | collective-permute-done | bytes 262176 | tf_op jit(solution)/shard_map/ppermute | solution.py:42
  67.7 3.0 %collective-permute-start.17 = (bf16[256,512]{1,0:T(8,128)(2,1)S(1)}, bf16[256,512]{1,0:T(8,128)(2,1)S(1)}, u32[]{:S(2)}, u32[]{:S(2)}) collective-permute-start(bf16[256,512]{1,0:T(8,128)(2,1)S(1)} %convolution_convert_fusion.7), channel_id=1, source_target_pairs={{0,57},{1,2},{2,1},{3,4},{4,3},{5,6},{6,5},{7,14},{8,11},{9,16},{1... | collective-permute-start | bytes 786440 | tf_op jit(solution)/shard_map/ppermute | solution.py:42
  71.2 3.6 %collective-permute-done.17 = bf16[256,512]{1,0:T(8,128)(2,1)S(1)} collective-permute-done((bf16[256,512]{1,0:T(8,128)(2,1)S(1)}, bf16[256,512]{1,0:T(8,128)(2,1)S(1)}, u32[]{:S(2)}, u32[]{:S(2)}) %collective-permute-start.17) | collective-permute-done | bytes 262176 | tf_op jit(solution)/shard_map/ppermute | solution.py:42
  76.4 3.0 %collective-permute-start.19 = (bf16[256,512]{1,0:T(8,128)(2,1)S(1)}, bf16[256,512]{1,0:T(8,128)(2,1)S(1)}, u32[]{:S(2)}, u32[]{:S(2)}) collective-permute-start(bf16[256,512]{1,0:T(8,128)(2,1)S(1)} %convolution_convert_fusion.6), channel_id=1, source_target_pairs={{0,57},{1,2},{2,1},{3,4},{4,3},{5,6},{6,5},{7,14},{8,11},{9,16},{1... | collective-permute-start | bytes 786440 | tf_op jit(solution)/shard_map/ppermute | solution.py:42
  80.5 3.0 %collective-permute-done.19 = bf16[256,512]{1,0:T(8,128)(2,1)S(1)} collective-permute-done((bf16[256,512]{1,0:T(8,128)(2,1)S(1)}, bf16[256,512]{1,0:T(8,128)(2,1)S(1)}, u32[]{:S(2)}, u32[]{:S(2)}) %collective-permute-start.19) | collective-permute-done | bytes 262176 | tf_op jit(solution)/shard_map/ppermute | solution.py:42
  85.7 6.0 %collective-permute-done.20 = bf16[256,512]{1,0:T(8,128)(2,1)S(1)} collective-permute-done((bf16[256,512]{1,0:T(8,128)(2,1)S(1)}, bf16[256,512]{1,0:T(8,128)(2,1)S(1)}, u32[]{:S(2)}, u32[]{:S(2)}) %collective-permute-start.20) | collective-permute-done | bytes 262176 | tf_op jit(solution)/shard_map/ppermute | solution.py:46
  92.8 3.0 %collective-permute-done.21 = bf16[256,1024]{1,0:T(8,128)(2,1)S(1)} collective-permute-done((bf16[256,1024]{1,0:T(8,128)(2,1)S(1)}, bf16[256,1024]{1,0:T(8,128)(2,1)S(1)}, u32[]{:S(2)}, u32[]{:S(2)}) %collective-permute-start.21) | collective-permute-done | bytes 524320 | tf_op jit(solution)/shard_map/ppermute | solution.py:46
  97.0 5.9 %collective-permute-done.23 = bf16[256,512]{1,0:T(8,128)(2,1)S(1)} collective-permute-done((bf16[256,512]{1,0:T(8,128)(2,1)S(1)}, bf16[256,512]{1,0:T(8,128)(2,1)S(1)}, u32[]{:S(2)}, u32[]{:S(2)}) %collective-permute-start.23) | collective-permute-done | bytes 262176 | tf_op jit(solution)/shard_map/ppermute | solution.py:42
  105.8 1.2 collective-permute-start.26
  107.0 4.4 %collective-permute-done.25 = bf16[256,512]{1,0:T(8,128)(2,1)S(1)} collective-permute-done((bf16[256,512]{1,0:T(8,128)(2,1)S(1)}, bf16[256,512]{1,0:T(8,128)(2,1)S(1)}, u32[]{:S(2)}, u32[]{:S(2)}) %collective-permute-start.25) | collective-permute-done | bytes 262176 | tf_op jit(solution)/shard_map/ppermute | solution.py:42
  112.6 2.2 %collective-permute-done.26 = bf16[256,512]{1,0:T(8,128)(2,1)S(1)} collective-permute-done((bf16[256,512]{1,0:T(8,128)(2,1)S(1)}, bf16[256,512]{1,0:T(8,128)(2,1)S(1)}, u32[]{:S(2)}, u32[]{:S(2)}) %collective-permute-start.26) | collective-permute-done | bytes 262176 | tf_op jit(solution)/shard_map/ppermute | solution.py:46
  117.8 4.7 %collective-permute-done.28 = bf16[256,512]{1,0:T(8,128)(2,1)S(1)} collective-permute-done((bf16[256,512]{1,0:T(8,128)(2,1)S(1)}, bf16[256,512]{1,0:T(8,128)(2,1)S(1)}, u32[]{:S(2)}, u32[]{:S(2)}) %collective-permute-start.28) | collective-permute-done | bytes 262176 | tf_op jit(solution)/shard_map/ppermute | solution.py:42
  127.2 1.4 collective-permute-start.35
  128.7 2.7 %collective-permute-start.36 = (bf16[32,3072]{1,0:T(8,128)(2,1)S(1)}, bf16[32,3072]{1,0:T(8,128)(2,1)S(1)}, u32[]{:S(2)}, u32[]{:S(2)}) collective-permute-start(bf16[32,3072]{1,0:T(8,128)(2,1)S(1)} %get-tuple-element.101), channel_id=1, source_target_pairs={{0,6},{1,7},{2,4},{3,5},{4,2},{5,3},{6,0},{7,1},{8,14},{9,15},{10,... | collective-permute-start | bytes 589832 | tf_op jit(solution)/shard_map/ppermute | solution.py:42
  131.3 1.4 collective-permute-done.30
  132.9 3.5 %collective-permute-done.34 = bf16[32,3072]{1,0:T(8,128)(2,1)S(1)} collective-permute-done((bf16[32,3072]{1,0:T(8,128)(2,1)S(1)}, bf16[32,3072]{1,0:T(8,128)(2,1)S(1)}, u32[]{:S(2)}, u32[]{:S(2)}) %collective-permute-start.34) | collective-permute-done | bytes 196640 | tf_op jit(solution)/shard_map/ppermute | solution.py:42
  136.5 4.1 %collective-permute-done.35 = bf16[32,3072]{1,0:T(8,128)(2,1)S(1)} collective-permute-done((bf16[32,3072]{1,0:T(8,128)(2,1)S(1)}, bf16[32,3072]{1,0:T(8,128)(2,1)S(1)}, u32[]{:S(2)}, u32[]{:S(2)}) %collective-permute-start.35) | collective-permute-done | bytes 196640 | tf_op jit(solution)/shard_map/ppermute | solution.py:42
  141.5 3.4 %all-to-all-start = ((bf16[8,4,3072]{2,1,0:T(4,128)(2,1)}), bf16[8,4,3072]{2,1,0:T(4,128)(2,1)S(1)}, u32[]{:S(2)}, u32[]{:S(2)}) async-start(bf16[8,4,3072]{2,1,0:T(4,128)(2,1)} %reshape.255), calls=%async_computation | async-start | bytes 393216 | tf_op jit(solution)/shard_map/all_to_all | solution.py:222
  144.9 2.1 %fusion.20 = bf16[256,512]{1,0:T(8,128)(2,1)} fusion(f32[256,512]{1,0:T(8,128)S(1)} %fusion.211, f32[256,512]{1,0:T(8,128)S(1)} %convolution_add_fusion.3, bf16[256,512]{1,0:T(8,128)(2,1)} %collective-permute-done.29, bf16[256,512]{1,0:T(8,128)(2,1)} %convolution_convert_fusion.2, f32[256,512]{1,0:T(8,128)S(1)} %get-tuple-element.125, ...), kind=kOutput, calls=%fused_computation.53 | convolution fusion | flops 136577024 | bytes 3407876 | tf_op jit(solution)/shard_map/dot_general | solution.py:67
  146.9 1.6 collective-permute-start.31
  148.5 6.8 %all-to-all-done = bf16[8,4,3072]{2,1,0:T(4,128)(2,1)S(1)} async-done(((bf16[8,4,3072]{2,1,0:T(4,128)(2,1)}), bf16[8,4,3072]{2,1,0:T(4,128)(2,1)S(1)}, u32[]{:S(2)}, u32[]{:S(2)}) %all-to-all-start) | async-done | bytes 196640 | tf_op jit(solution)/shard_map/all_to_all | solution.py:222
  156.5 2.2 %collective-permute-start.38 = (bf16[4,3072]{1,0:T(4,128)(2,1)S(1)}, bf16[4,3072]{1,0:T(4,128)(2,1)S(1)}, u32[]{:S(2)}, u32[]{:S(2)}) collective-permute-start(bf16[4,3072]{1,0:T(4,128)(2,1)S(1)} %reduce_sum.12), channel_id=1, source_target_pairs={{0,192},{64,128},{128,64},{192,0},{1,193},{65,129},{129,65},{193,1... | collective-permute-start | bytes 73736 | tf_op jit(solution)/shard_map/ppermute | solution.py:46
  161.5 2.5 %collective-permute-done.39 = bf16[4,3072]{1,0:T(4,128)(2,1)S(1)} collective-permute-done((bf16[4,3072]{1,0:T(4,128)(2,1)S(1)}, bf16[4,3072]{1,0:T(4,128)(2,1)S(1)}, u32[]{:S(2)}, u32[]{:S(2)}) %collective-permute-start.39) | collective-permute-done | bytes 24608 | tf_op jit(solution)/shard_map/ppermute | solution.py:46
  (171 shorter events, 40.7 us)
Async XLA Ops:
  3.2 13.6 %collective-permute-start.2 = (bf16[256,768]{0,1:T(8,128)(2,1)S(1)}, bf16[256,768]{0,1:T(8,128)(2,1)S(1)}, u32[]{:S(2)}, u32[]{:S(2)}) collective-permute-start(bf16[256,768]{0,1:T(8,128)(2,1)S(1)} %bitcast.73), channel_id=1, source_target_pairs={{0,0},{1,1},{2,2},{3,3},{4,4},{5,5},{6,6},{7,7},{14,8},{15,9},{12,... | collective-permute-start | bytes 1179656 | tf_op jit(solution)/shard_map/ppermute | solution.py:42
  4.0 12.8 %collective-permute-start.1 = (bf16[256,512]{1,0:T(8,128)(2,1)S(1)}, bf16[256,512]{1,0:T(8,128)(2,1)S(1)}, u32[]{:S(2)}, u32[]{:S(2)}) collective-permute-start(bf16[256,512]{1,0:T(8,128)(2,1)S(1)} %bitcast.74), channel_id=1, source_target_pairs={{0,0},{1,1},{2,2},{3,3},{4,4},{5,5},{6,6},{7,7},{14,8},{15,9},{12,... | collective-permute-start | bytes 786440 | tf_op jit(solution)/shard_map/ppermute | solution.py:42
  4.8 17.0 %collective-permute-start.4 = (bf16[256,512]{1,0:T(8,128)(2,1)S(1)}, bf16[256,512]{1,0:T(8,128)(2,1)S(1)}, u32[]{:S(2)}, u32[]{:S(2)}) collective-permute-start(bf16[256,512]{1,0:T(8,128)(2,1)S(1)} %bitcast.75), channel_id=1, source_target_pairs={{63,0},{2,1},{1,2},{4,3},{3,4},{6,5},{5,6},{8,7},{13,8},{16,9},{11... | collective-permute-start | bytes 786440 | tf_op jit(solution)/shard_map/ppermute | solution.py:42
  15.4 20.9 %collective-permute-start = (bf16[256,512]{1,0:T(8,128)(2,1)S(1)}, bf16[256,512]{1,0:T(8,128)(2,1)}, u32[]{:S(2)}, u32[]{:S(2)}) collective-permute-start(bf16[256,512]{1,0:T(8,128)(2,1)S(1)} %convert_element_type.177), channel_id=1, source_target_pairs={{0,0},{1,1},{2,2},{3,3},{4,4},{5,5},{6,6},{7,7},{14,8},{15,9},{12,... | collective-permute-start | bytes 786440 | tf_op jit(solution)/shard_map/ppermute | solution.py:42
  23.8 13.4 %collective-permute-start.6 = (bf16[256,512]{1,0:T(8,128)(2,1)S(1)}, bf16[256,512]{1,0:T(8,128)(2,1)S(1)}, u32[]{:S(2)}, u32[]{:S(2)}) collective-permute-start(bf16[256,512]{1,0:T(8,128)(2,1)S(1)} %convert_add_fusion.3), channel_id=1, source_target_pairs={{0,1},{1,0},{2,3},{3,2},{4,5},{5,4},{6,7},{7,6},{8,9},{9,8},{10,11... | collective-permute-start | bytes 786440 | tf_op jit(solution)/shard_map/ppermute | solution.py:42
  23.8 16.4 %collective-permute-start.7 = (bf16[256,512]{1,0:T(8,128)(2,1)S(1)}, bf16[256,512]{1,0:T(8,128)(2,1)S(1)}, u32[]{:S(2)}, u32[]{:S(2)}) collective-permute-start(bf16[256,512]{1,0:T(8,128)(2,1)S(1)} %convert_add_fusion.3), channel_id=1, source_target_pairs={{0,57},{1,2},{2,1},{3,4},{4,3},{5,6},{6,5},{7,14},{8,11},{9,16},{1... | collective-permute-start | bytes 786440 | tf_op jit(solution)/shard_map/ppermute | solution.py:42
  36.3 10.2 %collective-permute-start.5 = (bf16[256,512]{1,0:T(8,128)(2,1)}, bf16[256,512]{1,0:T(8,128)(2,1)S(1)}, u32[]{:S(2)}, u32[]{:S(2)}) collective-permute-start(bf16[256,512]{1,0:T(8,128)(2,1)} %collective-permute-done), channel_id=1, source_target_pairs={{0,64},{64,0},{128,192},{192,128},{1,65},{65,1},{129,193},{193,129... | collective-permute-start | bytes 786440 | tf_op jit(solution)/shard_map/ppermute | solution.py:46
  41.6 6.5 %collective-permute-start.8 = (bf16[256,512]{1,0:T(8,128)(2,1)S(1)}, bf16[256,512]{1,0:T(8,128)(2,1)S(1)}, u32[]{:S(2)}, u32[]{:S(2)}) collective-permute-start(bf16[256,512]{1,0:T(8,128)(2,1)S(1)} %get-tuple-element.112), channel_id=1, source_target_pairs={{0,64},{64,0},{128,192},{192,128},{1,65},{65,1},{129,193},{193,129... | collective-permute-start | bytes 786440 | tf_op jit(solution)/shard_map/ppermute | solution.py:46
  42.5 11.7 %collective-permute-start.11 = (bf16[256,256]{0,1:T(8,128)(2,1)S(1)}, bf16[256,256]{0,1:T(8,128)(2,1)S(1)}, u32[]{:S(2)}, u32[]{:S(2)}) collective-permute-start(bf16[256,256]{0,1:T(8,128)(2,1)S(1)} %get-tuple-element.118), channel_id=1, source_target_pairs={{0,57},{1,2},{2,1},{3,4},{4,3},{5,6},{6,5},{7,14},{8,11},{9,16},{1... | collective-permute-start | bytes 393224 | tf_op jit(solution)/shard_map/ppermute | solution.py:42
  45.3 13.0 %collective-permute-start.9 = (bf16[256,256]{0,1:T(8,128)(2,1)S(1)}, bf16[256,256]{0,1:T(8,128)(2,1)S(1)}, u32[]{:S(2)}, u32[]{:S(2)}) collective-permute-start(bf16[256,256]{0,1:T(8,128)(2,1)S(1)} %get-tuple-element.119), channel_id=1, source_target_pairs={{0,1},{1,0},{2,3},{3,2},{4,5},{5,4},{6,7},{7,6},{8,9},{9,8},{10,11... | collective-permute-start | bytes 393224 | tf_op jit(solution)/shard_map/ppermute | solution.py:42
  45.3 13.3 %collective-permute-start.13 = (bf16[256,512]{1,0:T(8,128)(2,1)S(1)}, bf16[256,512]{1,0:T(8,128)(2,1)S(1)}, u32[]{:S(2)}, u32[]{:S(2)}) collective-permute-start(bf16[256,512]{1,0:T(8,128)(2,1)S(1)} %get-tuple-element.39), channel_id=1, source_target_pairs={{0,64},{64,0},{128,192},{192,128},{1,65},{65,1},{129,193},{193,129... | collective-permute-start | bytes 786440 | tf_op jit(solution)/shard_map/ppermute | solution.py:46
  49.1 9.0 %collective-permute-start.12 = (bf16[256,512]{1,0:T(8,128)(2,1)S(1)}, bf16[256,512]{1,0:T(8,128)(2,1)S(1)}, u32[]{:S(2)}, u32[]{:S(2)}) collective-permute-start(bf16[256,512]{1,0:T(8,128)(2,1)S(1)} %convolution_convert_fusion.9), channel_id=1, source_target_pairs={{0,57},{1,2},{2,1},{3,4},{4,3},{5,6},{6,5},{7,14},{8,11},{9,16},{1... | collective-permute-start | bytes 786440 | tf_op jit(solution)/shard_map/ppermute | solution.py:42
  59.3 7.1 %collective-permute-start.15 = (bf16[256,512]{1,0:T(8,128)(2,1)S(1)}, bf16[256,512]{1,0:T(8,128)(2,1)S(1)}, u32[]{:S(2)}, u32[]{:S(2)}) collective-permute-start(bf16[256,512]{1,0:T(8,128)(2,1)S(1)} %convolution_convert_fusion.8), channel_id=1, source_target_pairs={{0,57},{1,2},{2,1},{3,4},{4,3},{5,6},{6,5},{7,14},{8,11},{9,16},{1... | collective-permute-start | bytes 786440 | tf_op jit(solution)/shard_map/ppermute | solution.py:42
  67.7 7.1 %collective-permute-start.17 = (bf16[256,512]{1,0:T(8,128)(2,1)S(1)}, bf16[256,512]{1,0:T(8,128)(2,1)S(1)}, u32[]{:S(2)}, u32[]{:S(2)}) collective-permute-start(bf16[256,512]{1,0:T(8,128)(2,1)S(1)} %convolution_convert_fusion.7), channel_id=1, source_target_pairs={{0,57},{1,2},{2,1},{3,4},{4,3},{5,6},{6,5},{7,14},{8,11},{9,16},{1... | collective-permute-start | bytes 786440 | tf_op jit(solution)/shard_map/ppermute | solution.py:42
  76.4 7.1 %collective-permute-start.19 = (bf16[256,512]{1,0:T(8,128)(2,1)S(1)}, bf16[256,512]{1,0:T(8,128)(2,1)S(1)}, u32[]{:S(2)}, u32[]{:S(2)}) collective-permute-start(bf16[256,512]{1,0:T(8,128)(2,1)S(1)} %convolution_convert_fusion.6), channel_id=1, source_target_pairs={{0,57},{1,2},{2,1},{3,4},{4,3},{5,6},{6,5},{7,14},{8,11},{9,16},{1... | collective-permute-start | bytes 786440 | tf_op jit(solution)/shard_map/ppermute | solution.py:42
  84.0 7.7 %collective-permute-start.20 = (bf16[256,512]{1,0:T(8,128)(2,1)S(1)}, bf16[256,512]{1,0:T(8,128)(2,1)S(1)}, u32[]{:S(2)}, u32[]{:S(2)}) collective-permute-start(bf16[256,512]{1,0:T(8,128)(2,1)S(1)} %fusion.8), channel_id=1, source_target_pairs={{0,192},{64,128},{128,64},{192,0},{1,193},{65,129},{129,65},{193,1... | collective-permute-start | bytes 786440 | tf_op jit(solution)/shard_map/ppermute | solution.py:46
  84.7 11.1 %collective-permute-start.21 = (bf16[256,1024]{1,0:T(8,128)(2,1)S(1)}, bf16[256,1024]{1,0:T(8,128)(2,1)S(1)}, u32[]{:S(2)}, u32[]{:S(2)}) collective-permute-start(bf16[256,1024]{1,0:T(8,128)(2,1)S(1)} %pad_maximum_fusion.1), channel_id=1, source_target_pairs={{0,64},{64,0},{128,192},{192,128},{1,65},{65,1},{129,193},{193,129... | collective-permute-start | bytes 1572872 | tf_op jit(solution)/shard_map/ppermute | solution.py:46
  95.9 7.1 %collective-permute-start.23 = (bf16[256,512]{1,0:T(8,128)(2,1)S(1)}, bf16[256,512]{1,0:T(8,128)(2,1)S(1)}, u32[]{:S(2)}, u32[]{:S(2)}) collective-permute-start(bf16[256,512]{1,0:T(8,128)(2,1)S(1)} %convolution_convert_fusion.5), channel_id=1, source_target_pairs={{0,57},{1,2},{2,1},{3,4},{4,3},{5,6},{6,5},{7,14},{8,11},{9,16},{1... | collective-permute-start | bytes 786440 | tf_op jit(solution)/shard_map/ppermute | solution.py:42
  96.9 6.3 %collective-permute-start.22 = (bf16[256,512]{1,0:T(8,128)(2,1)S(1)}, bf16[256,512]{1,0:T(8,128)(2,1)S(1)}, u32[]{:S(2)}, u32[]{:S(2)}) collective-permute-start(bf16[256,512]{1,0:T(8,128)(2,1)S(1)} %convolution_convert_fusion.5), channel_id=1, source_target_pairs={{0,1},{1,0},{2,3},{3,2},{4,5},{5,4},{6,7},{7,6},{8,9},{9,8},{10,11... | collective-permute-start | bytes 786440 | tf_op jit(solution)/shard_map/ppermute | solution.py:42
  104.3 7.1 %collective-permute-start.25 = (bf16[256,512]{1,0:T(8,128)(2,1)S(1)}, bf16[256,512]{1,0:T(8,128)(2,1)S(1)}, u32[]{:S(2)}, u32[]{:S(2)}) collective-permute-start(bf16[256,512]{1,0:T(8,128)(2,1)S(1)} %convolution_convert_fusion.4), channel_id=1, source_target_pairs={{0,57},{1,2},{2,1},{3,4},{4,3},{5,6},{6,5},{7,14},{8,11},{9,16},{1... | collective-permute-start | bytes 786440 | tf_op jit(solution)/shard_map/ppermute | solution.py:42
  105.6 5.9 %collective-permute-start.24 = (bf16[256,512]{1,0:T(8,128)(2,1)S(1)}, bf16[256,512]{1,0:T(8,128)(2,1)S(1)}, u32[]{:S(2)}, u32[]{:S(2)}) collective-permute-start(bf16[256,512]{1,0:T(8,128)(2,1)S(1)} %convolution_convert_fusion.4), channel_id=1, source_target_pairs={{0,1},{1,0},{2,3},{3,2},{4,5},{5,4},{6,7},{7,6},{8,9},{9,8},{10,11... | collective-permute-start | bytes 786440 | tf_op jit(solution)/shard_map/ppermute | solution.py:42
  105.8 9.0 %collective-permute-start.26 = (bf16[256,512]{1,0:T(8,128)(2,1)S(1)}, bf16[256,512]{1,0:T(8,128)(2,1)S(1)}, u32[]{:S(2)}, u32[]{:S(2)}) collective-permute-start(bf16[256,512]{1,0:T(8,128)(2,1)S(1)} %pad_maximum_fusion.5), channel_id=1, source_target_pairs={{0,64},{64,0},{128,192},{192,128},{1,65},{65,1},{129,193},{193,129... | collective-permute-start | bytes 786440 | tf_op jit(solution)/shard_map/ppermute | solution.py:46
  115.4 7.1 %collective-permute-start.28 = (bf16[256,512]{1,0:T(8,128)(2,1)S(1)}, bf16[256,512]{1,0:T(8,128)(2,1)S(1)}, u32[]{:S(2)}, u32[]{:S(2)}) collective-permute-start(bf16[256,512]{1,0:T(8,128)(2,1)S(1)} %convolution_convert_fusion.3), channel_id=1, source_target_pairs={{0,57},{1,2},{2,1},{3,4},{4,3},{5,6},{6,5},{7,14},{8,11},{9,16},{1... | collective-permute-start | bytes 786440 | tf_op jit(solution)/shard_map/ppermute | solution.py:42
  116.7 10.1 %collective-permute-start.33 = (bf16[128,1536]{1,0:T(8,128)(2,1)S(1)}, bf16[128,1536]{1,0:T(8,128)(2,1)S(1)}, u32[]{:S(2)}, u32[]{:S(2)}) collective-permute-start(bf16[128,1536]{1,0:T(8,128)(2,1)S(1)} %pad_maximum_fusion.3), channel_id=1, source_target_pairs={{0,1},{1,0},{2,3},{3,2},{4,5},{5,4},{6,7},{7,6},{8,9},{9,8},{10,11... | collective-permute-start | bytes 1179656 | tf_op jit(solution)/shard_map/ppermute | solution.py:42
  117.2 5.5 %collective-permute-start.27 = (bf16[256,512]{1,0:T(8,128)(2,1)S(1)}, bf16[256,512]{1,0:T(8,128)(2,1)S(1)}, u32[]{:S(2)}, u32[]{:S(2)}) collective-permute-start(bf16[256,512]{1,0:T(8,128)(2,1)S(1)} %convolution_convert_fusion.3), channel_id=1, source_target_pairs={{0,1},{1,0},{2,3},{3,2},{4,5},{5,4},{6,7},{7,6},{8,9},{9,8},{10,11... | collective-permute-start | bytes 786440 | tf_op jit(solution)/shard_map/ppermute | solution.py:42
  125.5 7.2 %collective-permute-start.30 = (bf16[256,512]{1,0:T(8,128)(2,1)}, bf16[256,512]{1,0:T(8,128)(2,1)S(1)}, u32[]{:S(2)}, u32[]{:S(2)}) collective-permute-start(bf16[256,512]{1,0:T(8,128)(2,1)} %convolution_convert_fusion.2), channel_id=1, source_target_pairs={{0,57},{1,2},{2,1},{3,4},{4,3},{5,6},{6,5},{7,14},{8,11},{9,16},{1... | collective-permute-start | bytes 786440 | tf_op jit(solution)/shard_map/ppermute | solution.py:42
  126.6 18.2 %collective-permute-start.29 = (bf16[256,512]{1,0:T(8,128)(2,1)}, bf16[256,512]{1,0:T(8,128)(2,1)}, u32[]{:S(2)}, u32[]{:S(2)}) collective-permute-start(bf16[256,512]{1,0:T(8,128)(2,1)} %convolution_convert_fusion.2), channel_id=1, source_target_pairs={{0,1},{1,0},{2,3},{3,2},{4,5},{5,4},{6,7},{7,6},{8,9},{9,8},{10,11... | collective-permute-start | bytes 786440 | tf_op jit(solution)/shard_map/ppermute | solution.py:42
  127.1 9.3 %collective-permute-start.34 = (bf16[32,3072]{1,0:T(8,128)(2,1)S(1)}, bf16[32,3072]{1,0:T(8,128)(2,1)S(1)}, u32[]{:S(2)}, u32[]{:S(2)}) collective-permute-start(bf16[32,3072]{1,0:T(8,128)(2,1)S(1)} %get-tuple-element.100), channel_id=1, source_target_pairs={{0,4},{1,5},{2,6},{3,7},{4,0},{5,1},{6,2},{7,3},{8,12},{9,13},{10,... | collective-permute-start | bytes 589832 | tf_op jit(solution)/shard_map/ppermute | solution.py:42
  127.2 13.4 %collective-permute-start.35 = (bf16[32,3072]{1,0:T(8,128)(2,1)S(1)}, bf16[32,3072]{1,0:T(8,128)(2,1)S(1)}, u32[]{:S(2)}, u32[]{:S(2)}) collective-permute-start(bf16[32,3072]{1,0:T(8,128)(2,1)S(1)} %get-tuple-element.102), channel_id=1, source_target_pairs={{0,2},{1,3},{2,0},{3,1},{4,6},{5,7},{6,4},{7,5},{8,10},{9,11},{10,... | collective-permute-start | bytes 589832 | tf_op jit(solution)/shard_map/ppermute | solution.py:42
  128.7 11.9 %collective-permute-start.36 = (bf16[32,3072]{1,0:T(8,128)(2,1)S(1)}, bf16[32,3072]{1,0:T(8,128)(2,1)S(1)}, u32[]{:S(2)}, u32[]{:S(2)}) collective-permute-start(bf16[32,3072]{1,0:T(8,128)(2,1)S(1)} %get-tuple-element.101), channel_id=1, source_target_pairs={{0,6},{1,7},{2,4},{3,5},{4,2},{5,3},{6,0},{7,1},{8,14},{9,15},{10,... | collective-permute-start | bytes 589832 | tf_op jit(solution)/shard_map/ppermute | solution.py:42
  141.5 13.9 %all-to-all-start = ((bf16[8,4,3072]{2,1,0:T(4,128)(2,1)}), bf16[8,4,3072]{2,1,0:T(4,128)(2,1)S(1)}, u32[]{:S(2)}, u32[]{:S(2)}) async-start(bf16[8,4,3072]{2,1,0:T(4,128)(2,1)} %reshape.255), calls=%async_computation | async-start | bytes 393216 | tf_op jit(solution)/shard_map/all_to_all | solution.py:222
  146.9 12.9 %collective-permute-start.31 = (bf16[256,512]{1,0:T(8,128)(2,1)}, bf16[256,512]{1,0:T(8,128)(2,1)S(1)}, u32[]{:S(2)}, u32[]{:S(2)}) collective-permute-start(bf16[256,512]{1,0:T(8,128)(2,1)} %fusion.20), channel_id=1, source_target_pairs={{0,0},{1,1},{2,2},{3,3},{4,4},{5,5},{6,6},{7,7},{14,8},{15,9},{12,... | collective-permute-start | bytes 786440 | tf_op jit(solution)/shard_map/ppermute | solution.py:42
  (20 other events, 100.3 us)
where the time goes:
time: 165 us
  waiting for transfers between devices  67.3 us (41%)
  starting transfers between devices  67.1 us (41%)
  matrix products  21.3 us (13%)
  other arithmetic  4.33 us (3%)
  between operations  2.42 us (1%)
  local copies, waits for them, and re-layouts  2.19 us (1%)
    ppermute x31, starting transfers between devices, over_node(): return lax.ppermute(value, 'node', pairs)  53.6 us
    ppermute x31, waiting for transfers between devices, over_node(): return lax.ppermute(value, 'node', pairs)  45.5 us
    ppermute x9, waiting for transfers between devices, over_step(): return lax.ppermute(value, 'step', [(s, s ^ k) for s in range(STEPS)])  15 us
    ppermute x9, starting transfers between devices, over_step(): return lax.ppermute(value, 'step', [(s, s ^ k) for s in range(STEPS)])  10.1 us
    dot_general x24, matrix products, mul_t(): lax.dot_general(left, right, (((1,), (1,)), ((), ())), preferred_element_...  8.98 us
    dot_general x20, matrix products, t_mul(): lax.dot_general(left, right, (((0,), (0,)), ((), ())), preferred_element_...  7.53 us
    all_to_all x1, waiting for transfers between devices, on_device(): lax.all_to_all(sent, 'node', 0, 0, axis_index_groups=Z_GROUPS, tiled=False)  6.85 us
    dot_general x12, matrix products, mul(): return jnp.dot(left, right, preferred_element_type=F32)  4.36 us
  transfers between devices with their start and end apart: 41, of which 19 were waited for; matrix products, arithmetic and copies ran while one was open for 12% of the time, Pallas kernels for 0%

commit v1 on v0

--- a/solution.py
+++ b/solution.py
@@ -124,9 +124,10 @@
             hb = h.astype(BF16)
             outer = over_node(hb, OUTER)
         sib = over_node(hb, SIBLING)
-        local = mul(m_own, hb)
+        local = mul(m_own, hb) + mul(m_sib, sib)
         first = mul(hb, wa)
-        mb = (local + mul(m_sib, sib) + mul(m_out, outer)).astype(BF16)
+        local, outer = lax.optimization_barrier((local, outer))
+        mb = (local + mul(m_out, outer)).astype(BF16)
         zz = first + mul(mb, wb)
         sig = jax.nn.sigmoid(zz)
         g = (zz * sig).astype(BF16)
@@ -150,7 +151,7 @@
     upper = x >= 2
     share = width // SPLIT
     choice = feature_choice(width, x, yi, ci, width // NODES // SPLIT)
-    crossing = {(1, 0): [3, 4, 5, 0], (2, 0): [1, 2]}
+    crossing = {(0, 0): [3, 4], (1, 0): [5, 0, 1, 2]}
 
     def sum_rows(layer):
         pairs = [
@@ -208,7 +209,9 @@
                 kept[turn, layer] = after((ab, dzb), dm)
                 keep, sent = split_cores(sum_rows(layer))
                 grads[layer] = keep + over_node(sent, SIBLING).astype(F32)
-            adjoint = adjoint + t_mul(n_chip, jnp.concatenate([dm, d_sib], axis=0)) + t_mul(n_out, d_out)
+            adjoint = adjoint + t_mul(n_chip, jnp.concatenate([dm, d_sib], axis=0))
+            adjoint, d_out = lax.optimization_barrier((adjoint, d_out))
+            adjoint = adjoint + t_mul(n_out, d_out)
         result = jnp.where(x == STEPS - 1 - turn, adjoint, result)
     result = over_node(result.astype(BF16), FLIP).astype(F32)
 

time: 165 us -> 186 us (1.13)
  waiting for transfers between devices: 67.3 us -> 91.7 us
  starting transfers between devices: 67.1 us -> 49.9 us
  matrix products: 21.3 us -> 28.6 us
  other arithmetic: 4.33 us -> 9.09 us
    ppermute x31, waiting for transfers between devices: 45.5 us -> 63.2 us  [over_node(): return lax.ppermute(value, 'node', pairs)]
    ppermute x31, starting transfers between devices: 53.6 us -> 38.5 us  [over_node(): return lax.ppermute(value, 'node', pairs)]
    dot_general x24, matrix products: 8.98 us -> 12.6 us  [mul_t(): lax.dot_general(left, right, (((1,), (1,)), ((), ())), preferred_element_...]
    ppermute x9, waiting for transfers between devices: 15 us -> 18.6 us  [over_step(): return lax.ppermute(value, 'step', [(s, s ^ k) for s in range(STEPS)])]
    select_n x2, other arithmetic: 0.15 us -> 3.28 us  [of_turn(): jnp.where(own_first, own, other)]
    all_to_all x1, waiting for transfers between devices: 6.85 us -> 9.96 us  [on_device(): lax.all_to_all(sent, 'node', 0, 0, axis_index_groups=Z_GROUPS, tiled=False)]
    dot_general x20, matrix products: 7.53 us -> 10.5 us  [t_mul(): lax.dot_general(left, right, (((0,), (0,)), ((), ())), preferred_element_...]
    ppermute x9, starting transfers between devices: 10.1 us -> 8.04 us  [over_step(): return lax.ppermute(value, 'step', [(s, s ^ k) for s in range(STEPS)])]
  transfers between devices with their start and end apart: 41 -> 41, of which waited for: 19 -> 28; matrix products, arithmetic and copies ran while one was open for 12% -> 13% of each run, Pallas kernels for 0% -> 0%
where the time goes in v1:
time: 186 us; the launch traced here: 185 us
  waiting for transfers between devices  91.7 us (49%)
  starting transfers between devices  49.9 us (27%)
  matrix products  28.6 us (15%)
  other arithmetic  9.09 us (5%)
  local copies, waits for them, and re-layouts  3.47 us (2%)
  between operations  2.71 us (1%)
    ppermute x31, waiting for transfers between devices, over_node(): return lax.ppermute(value, 'node', pairs)  63.2 us
    ppermute x31, starting transfers between devices, over_node(): return lax.ppermute(value, 'node', pairs)  38.5 us
    ppermute x9, waiting for transfers between devices, over_step(): return lax.ppermute(value, 'step', [(s, s ^ k) for s in range(STEPS)])  18.6 us
    dot_general x24, matrix products, mul_t(): lax.dot_general(left, right, (((1,), (1,)), ((), ())), preferred_element_...  12.6 us
    dot_general x20, matrix products, t_mul(): lax.dot_general(left, right, (((0,), (0,)), ((), ())), preferred_element_...  10.5 us
    all_to_all x1, waiting for transfers between devices, on_device(): lax.all_to_all(sent, 'node', 0, 0, axis_index_groups=Z_GROUPS, tiled=False)  9.96 us
    ppermute x9, starting transfers between devices, over_step(): return lax.ppermute(value, 'step', [(s, s ^ k) for s in range(STEPS)])  8.04 us
    dot_general x12, matrix products, mul(): return jnp.dot(left, right, preferred_element_type=F32)  5.08 us
  transfers between devices with their start and end apart: 41, of which 28 were waited for; matrix products, arithmetic and copies ran while one was open for 13% of the time, Pallas kernels for 0%

profile of v1, /device:TPU:6, one launch (start us, length us, event | category | flops | bytes accessed | tf_op | source)
XLA Modules:
  0.0 185.4 jit_solution(2876038252767396237)
XLA Ops:
  4.9 24.1 %collective-permute-start.4 = (bf16[256,512]{1,0:T(8,128)(2,1)S(1)}, bf16[256,512]{1,0:T(8,128)(2,1)S(1)}, u32[]{:S(2)}, u32[]{:S(2)}) collective-permute-start(bf16[256,512]{1,0:T(8,128)(2,1)S(1)} %bitcast.79), channel_id=1, source_target_pairs={{63,0},{2,1},{1,2},{4,3},{3,4},{6,5},{5,6},{8,7},{13,8},{16,9},{11... | collective-permute-start | bytes 786440 | tf_op jit(solution)/shard_map/ppermute | solution.py:42
  29.1 1.3 collective-permute-start
  30.9 4.5 %collective-permute-done.4 = bf16[256,512]{1,0:T(8,128)(2,1)S(1)} collective-permute-done((bf16[256,512]{1,0:T(8,128)(2,1)S(1)}, bf16[256,512]{1,0:T(8,128)(2,1)S(1)}, u32[]{:S(2)}, u32[]{:S(2)}) %collective-permute-start.4) | collective-permute-done | bytes 262176 | tf_op jit(solution)/shard_map/ppermute | solution.py:42
  40.2 4.7 %collective-permute-done.7 = bf16[256,512]{1,0:T(8,128)(2,1)S(1)} collective-permute-done((bf16[256,512]{1,0:T(8,128)(2,1)S(1)}, bf16[256,512]{1,0:T(8,128)(2,1)S(1)}, u32[]{:S(2)}, u32[]{:S(2)}) %collective-permute-start.7) | collective-permute-done | bytes 262176 | tf_op jit(solution)/shard_map/ppermute | solution.py:42
  47.8 1.2 collective-permute-start.13
  50.0 5.4 %collective-permute-done.8 = bf16[256,512]{1,0:T(8,128)(2,1)S(1)} collective-permute-done((bf16[256,512]{1,0:T(8,128)(2,1)S(1)}, bf16[256,512]{1,0:T(8,128)(2,1)S(1)}, u32[]{:S(2)}, u32[]{:S(2)}) %collective-permute-start.8) | collective-permute-done | bytes 262176 | tf_op jit(solution)/shard_map/ppermute | solution.py:46
  58.7 4.9 %collective-permute-done.11 = bf16[256,512]{1,0:T(8,128)(2,1)S(1)} collective-permute-done((bf16[256,512]{1,0:T(8,128)(2,1)S(1)}, bf16[256,512]{1,0:T(8,128)(2,1)S(1)}, u32[]{:S(2)}, u32[]{:S(2)}) %collective-permute-start.11) | collective-permute-done | bytes 262176 | tf_op jit(solution)/shard_map/ppermute | solution.py:42
  63.8 1.5 fusion.2
  67.9 5.3 %collective-permute-done.15 = bf16[256,512]{1,0:T(8,128)(2,1)S(1)} collective-permute-done((bf16[256,512]{1,0:T(8,128)(2,1)S(1)}, bf16[256,512]{1,0:T(8,128)(2,1)S(1)}, u32[]{:S(2)}, u32[]{:S(2)}) %collective-permute-start.15) | collective-permute-done | bytes 262176 | tf_op jit(solution)/shard_map/ppermute | solution.py:42
  77.6 5.2 %collective-permute-done.18 = bf16[256,512]{1,0:T(8,128)(2,1)S(1)} collective-permute-done((bf16[256,512]{1,0:T(8,128)(2,1)S(1)}, bf16[256,512]{1,0:T(8,128)(2,1)S(1)}, u32[]{:S(2)}, u32[]{:S(2)}) %collective-permute-start.18) | collective-permute-done | bytes 262176 | tf_op jit(solution)/shard_map/ppermute | solution.py:42
  85.4 1.4 collective-permute-done.19
  86.8 1.3 convolution_add_fusion.10
  88.1 4.2 %collective-permute-done.20 = bf16[256,512]{1,0:T(8,128)(2,1)} collective-permute-done((bf16[256,512]{1,0:T(8,128)(2,1)}, bf16[256,512]{1,0:T(8,128)(2,1)}, u32[]{:S(2)}, u32[]{:S(2)}) %collective-permute-start.20) | collective-permute-done | bytes 262176 | tf_op jit(solution)/shard_map/ppermute | solution.py:42
  92.3 2.0 %add_convert_fusion.4 = (bf16[256,512]{1,0:T(8,128)(2,1)S(1)}, f32[256,512]{1,0:T(8,128)}) fusion(f32[256,512]{1,0:T(8,128)S(1)} %convolution_add_fusion.10, bf16[256,256]{0,1:T(8,128)(2,1)S(1)} %collective-permute-done.12, bf16[256,512]{1,0:T(8,128)(2,1)} %collective-permute-done.20), kind=kOutput, calls=%fused_computation.193 | convolution fusion | flops 67371008 | bytes 1703936 | tf_op jit(solution)/shard_map/dot_general | solution.py:67
  95.5 2.1 %broadcast_select_fusion.19 = (bf16[256,256]{1,0:T(8,128)(2,1)}, bf16[256,256]{1,0:T(8,128)(2,1)}, bf16[256,256]{1,0:T(8,128)(2,1)S(1)}, bf16[256,256]{1,0:T(8,1...) fusion(bf16[256,256]{1,0:T(8,128)(2,1)} %get-tuple-element.105,, ...), kind=kLoop, calls=%fused_computation.201 | loop fusion | flops 262144 | bytes 2097153 | tf_op jit(solution)/shard_map/jit(_where)/select_n | solution.py:149
  97.9 5.3 %collective-permute-done.21 = bf16[256,512]{1,0:T(8,128)(2,1)S(1)} collective-permute-done((bf16[256,512]{1,0:T(8,128)(2,1)S(1)}, bf16[256,512]{1,0:T(8,128)(2,1)S(1)}, u32[]{:S(2)}, u32[]{:S(2)}) %collective-permute-start.21) | collective-permute-done | bytes 262176 | tf_op jit(solution)/shard_map/ppermute | solution.py:46
  105.7 5.1 %collective-permute-done.22 = bf16[256,1024]{1,0:T(8,128)(2,1)S(1)} collective-permute-done((bf16[256,1024]{1,0:T(8,128)(2,1)S(1)}, bf16[256,1024]{1,0:T(8,128)(2,1)S(1)}, u32[]{:S(2)}, u32[]{:S(2)}) %collective-permute-start.22) | collective-permute-done | bytes 524320 | tf_op jit(solution)/shard_map/ppermute | solution.py:46
  113.7 1.3 convolution_add_fusion.8
  115.1 4.1 %collective-permute-done.24 = bf16[256,512]{1,0:T(8,128)(2,1)S(1)} collective-permute-done((bf16[256,512]{1,0:T(8,128)(2,1)}, bf16[256,512]{1,0:T(8,128)(2,1)S(1)}, u32[]{:S(2)}, u32[]{:S(2)}) %collective-permute-start.24) | collective-permute-done | bytes 262176 | tf_op jit(solution)/shard_map/ppermute | solution.py:42
  120.4 1.4 broadcast_select_fusion.7
  125.1 4.5 %collective-permute-done.26 = bf16[256,512]{1,0:T(8,128)(2,1)S(1)} collective-permute-done((bf16[256,512]{1,0:T(8,128)(2,1)S(1)}, bf16[256,512]{1,0:T(8,128)(2,1)S(1)}, u32[]{:S(2)}, u32[]{:S(2)}) %collective-permute-start.26) | collective-permute-done | bytes 262176 | tf_op jit(solution)/shard_map/ppermute | solution.py:42
  133.7 4.0 %collective-permute-done.28 = bf16[256,512]{1,0:T(8,128)(2,1)S(1)} collective-permute-done((bf16[256,512]{1,0:T(8,128)(2,1)S(1)}, bf16[256,512]{1,0:T(8,128)(2,1)S(1)}, u32[]{:S(2)}, u32[]{:S(2)}) %collective-permute-start.28) | collective-permute-done | bytes 262176 | tf_op jit(solution)/shard_map/ppermute | solution.py:42
  141.8 5.3 %collective-permute-done.30 = bf16[256,512]{1,0:T(8,128)(2,1)S(1)} collective-permute-done((bf16[256,512]{1,0:T(8,128)(2,1)S(1)}, bf16[256,512]{1,0:T(8,128)(2,1)S(1)}, u32[]{:S(2)}, u32[]{:S(2)}) %collective-permute-start.30) | collective-permute-done | bytes 262176 | tf_op jit(solution)/shard_map/ppermute | solution.py:42
  148.5 1.6 collective-permute-done.33
  150.4 1.8 collective-permute-start.36
  152.3 1.7 collective-permute-start.35
  153.9 5.8 %collective-permute-done.34 = bf16[32,3072]{1,0:T(8,128)(2,1)S(1)} collective-permute-done((bf16[32,3072]{1,0:T(8,128)(2,1)S(1)}, bf16[32,3072]{1,0:T(8,128)(2,1)S(1)}, u32[]{:S(2)}, u32[]{:S(2)}) %collective-permute-start.34) | collective-permute-done | bytes 196640 | tf_op jit(solution)/shard_map/ppermute | solution.py:42
  159.7 3.2 %collective-permute-done.36 = bf16[32,3072]{1,0:T(8,128)(2,1)S(1)} collective-permute-done((bf16[32,3072]{1,0:T(8,128)(2,1)S(1)}, bf16[32,3072]{1,0:T(8,128)(2,1)S(1)}, u32[]{:S(2)}, u32[]{:S(2)}) %collective-permute-start.36) | collective-permute-done | bytes 196640 | tf_op jit(solution)/shard_map/ppermute | solution.py:42
  163.8 3.4 %all-to-all-start = ((bf16[8,4,3072]{2,1,0:T(4,128)(2,1)}), bf16[8,4,3072]{2,1,0:T(4,128)(2,1)S(1)}, u32[]{:S(2)}, u32[]{:S(2)}) async-start(bf16[8,4,3072]{2,1,0:T(4,128)(2,1)} %reshape.255), calls=%async_computation | async-start | bytes 393216 | tf_op jit(solution)/shard_map/all_to_all | solution.py:225
  167.9 10.0 %all-to-all-done = bf16[8,4,3072]{2,1,0:T(4,128)(2,1)S(1)} async-done(((bf16[8,4,3072]{2,1,0:T(4,128)(2,1)}), bf16[8,4,3072]{2,1,0:T(4,128)(2,1)S(1)}, u32[]{:S(2)}, u32[]{:S(2)}) %all-to-all-start) | async-done | bytes 196640 | tf_op jit(solution)/shard_map/all_to_all | solution.py:225
  177.9 1.3 collective-permute-start.39
  179.2 1.7 collective-permute-start.38
  (226 shorter events, 52.3 us)
Async XLA Ops:
  3.2 27.3 %collective-permute-start.2 = (bf16[256,768]{0,1:T(8,128)(2,1)S(1)}, bf16[256,768]{0,1:T(8,128)(2,1)S(1)}, u32[]{:S(2)}, u32[]{:S(2)}) collective-permute-start(bf16[256,768]{0,1:T(8,128)(2,1)S(1)} %bitcast.77), channel_id=1, source_target_pairs={{0,0},{1,1},{2,2},{3,3},{4,4},{5,5},{6,6},{7,7},{14,8},{15,9},{12,... | collective-permute-start | bytes 1179656 | tf_op jit(solution)/shard_map/ppermute | solution.py:42
  4.8 25.9 %collective-permute-start.3 = (bf16[256,512]{1,0:T(8,128)(2,1)S(1)}, bf16[256,512]{1,0:T(8,128)(2,1)S(1)}, u32[]{:S(2)}, u32[]{:S(2)}) collective-permute-start(bf16[256,512]{1,0:T(8,128)(2,1)S(1)} %collective-permute-done.1), channel_id=1, source_target_pairs={{0,1},{1,0},{2,3},{3,2},{4,5},{5,4},{6,7},{7,6},{8,9},{9,8},{10,11... | collective-permute-start | bytes 786440 | tf_op jit(solution)/shard_map/ppermute | solution.py:42
  4.9 30.6 %collective-permute-start.4 = (bf16[256,512]{1,0:T(8,128)(2,1)S(1)}, bf16[256,512]{1,0:T(8,128)(2,1)S(1)}, u32[]{:S(2)}, u32[]{:S(2)}) collective-permute-start(bf16[256,512]{1,0:T(8,128)(2,1)S(1)} %bitcast.79), channel_id=1, source_target_pairs={{63,0},{2,1},{1,2},{4,3},{3,4},{6,5},{5,6},{8,7},{13,8},{16,9},{11... | collective-permute-start | bytes 786440 | tf_op jit(solution)/shard_map/ppermute | solution.py:42
  29.1 9.8 %collective-permute-start = (bf16[256,512]{1,0:T(8,128)(2,1)S(1)}, bf16[256,512]{1,0:T(8,128)(2,1)}, u32[]{:S(2)}, u32[]{:S(2)}) collective-permute-start(bf16[256,512]{1,0:T(8,128)(2,1)S(1)} %convert_element_type.177), channel_id=1, source_target_pairs={{0,0},{1,1},{2,2},{3,3},{4,4},{5,5},{6,6},{7,7},{14,8},{15,9},{12,... | collective-permute-start | bytes 786440 | tf_op jit(solution)/shard_map/ppermute | solution.py:42
  37.6 2.1 %collective-permute-start.6 = (bf16[256,512]{1,0:T(8,128)(2,1)S(1)}, bf16[256,512]{1,0:T(8,128)(2,1)S(1)}, u32[]{:S(2)}, u32[]{:S(2)}) collective-permute-start(bf16[256,512]{1,0:T(8,128)(2,1)S(1)} %convert_add_fusion.3), channel_id=1, source_target_pairs={{0,1},{1,0},{2,3},{3,2},{4,5},{5,4},{6,7},{7,6},{8,9},{9,8},{10,11... | collective-permute-start | bytes 786440 | tf_op jit(solution)/shard_map/ppermute | solution.py:42
  37.8 7.1 %collective-permute-start.7 = (bf16[256,512]{1,0:T(8,128)(2,1)S(1)}, bf16[256,512]{1,0:T(8,128)(2,1)S(1)}, u32[]{:S(2)}, u32[]{:S(2)}) collective-permute-start(bf16[256,512]{1,0:T(8,128)(2,1)S(1)} %convert_add_fusion.3), channel_id=1, source_target_pairs={{0,57},{1,2},{2,1},{3,4},{4,3},{5,6},{6,5},{7,14},{8,11},{9,16},{1... | collective-permute-start | bytes 786440 | tf_op jit(solution)/shard_map/ppermute | solution.py:42
  38.9 10.1 %collective-permute-start.5 = (bf16[256,512]{1,0:T(8,128)(2,1)}, bf16[256,512]{1,0:T(8,128)(2,1)S(1)}, u32[]{:S(2)}, u32[]{:S(2)}) collective-permute-start(bf16[256,512]{1,0:T(8,128)(2,1)} %collective-permute-done), channel_id=1, source_target_pairs={{0,64},{64,0},{128,192},{192,128},{1,65},{65,1},{129,193},{193,129... | collective-permute-start | bytes 786440 | tf_op jit(solution)/shard_map/ppermute | solution.py:46
  46.1 9.3 %collective-permute-start.8 = (bf16[256,512]{1,0:T(8,128)(2,1)S(1)}, bf16[256,512]{1,0:T(8,128)(2,1)S(1)}, u32[]{:S(2)}, u32[]{:S(2)}) collective-permute-start(bf16[256,512]{1,0:T(8,128)(2,1)S(1)} %get-tuple-element.158), channel_id=1, source_target_pairs={{0,64},{64,0},{128,192},{192,128},{1,65},{65,1},{129,193},{193,129... | collective-permute-start | bytes 786440 | tf_op jit(solution)/shard_map/ppermute | solution.py:46
  47.0 16.5 %collective-permute-start.12 = (bf16[256,256]{0,1:T(8,128)(2,1)S(1)}, bf16[256,256]{0,1:T(8,128)(2,1)S(1)}, u32[]{:S(2)}, u32[]{:S(2)}) collective-permute-start(bf16[256,256]{0,1:T(8,128)(2,1)S(1)} %get-tuple-element.163), channel_id=1, source_target_pairs={{0,57},{1,2},{2,1},{3,4},{4,3},{5,6},{6,5},{7,14},{8,11},{9,16},{1... | collective-permute-start | bytes 393224 | tf_op jit(solution)/shard_map/ppermute | solution.py:42
  47.8 10.3 %collective-permute-start.9 = (bf16[256,256]{0,1:T(8,128)(2,1)S(1)}, bf16[256,256]{0,1:T(8,128)(2,1)S(1)}, u32[]{:S(2)}, u32[]{:S(2)}) collective-permute-start(bf16[256,256]{0,1:T(8,128)(2,1)S(1)} %get-tuple-element.164), channel_id=1, source_target_pairs={{0,1},{1,0},{2,3},{3,2},{4,5},{5,4},{6,7},{7,6},{8,9},{9,8},{10,11... | collective-permute-start | bytes 393224 | tf_op jit(solution)/shard_map/ppermute | solution.py:42
  47.8 16.0 %collective-permute-start.13 = (bf16[256,512]{1,0:T(8,128)(2,1)}, bf16[256,512]{1,0:T(8,128)(2,1)S(1)}, u32[]{:S(2)}, u32[]{:S(2)}) collective-permute-start(bf16[256,512]{1,0:T(8,128)(2,1)} %get-tuple-element.65), channel_id=1, source_target_pairs={{0,64},{64,0},{128,192},{192,128},{1,65},{65,1},{129,193},{193,129... | collective-permute-start | bytes 786440 | tf_op jit(solution)/shard_map/ppermute | solution.py:46
  56.4 7.1 %collective-permute-start.11 = (bf16[256,512]{1,0:T(8,128)(2,1)S(1)}, bf16[256,512]{1,0:T(8,128)(2,1)S(1)}, u32[]{:S(2)}, u32[]{:S(2)}) collective-permute-start(bf16[256,512]{1,0:T(8,128)(2,1)S(1)} %convolution_convert_fusion.9), channel_id=1, source_target_pairs={{0,57},{1,2},{2,1},{3,4},{4,3},{5,6},{6,5},{7,14},{8,11},{9,16},{1... | collective-permute-start | bytes 786440 | tf_op jit(solution)/shard_map/ppermute | solution.py:42
  66.1 7.1 %collective-permute-start.15 = (bf16[256,512]{1,0:T(8,128)(2,1)S(1)}, bf16[256,512]{1,0:T(8,128)(2,1)S(1)}, u32[]{:S(2)}, u32[]{:S(2)}) collective-permute-start(bf16[256,512]{1,0:T(8,128)(2,1)S(1)} %convolution_convert_fusion.8), channel_id=1, source_target_pairs={{0,57},{1,2},{2,1},{3,4},{4,3},{5,6},{6,5},{7,14},{8,11},{9,16},{1... | collective-permute-start | bytes 786440 | tf_op jit(solution)/shard_map/ppermute | solution.py:42
  66.4 8.7 %collective-permute-start.16 = (bf16[256,512]{1,0:T(8,128)(2,1)S(1)}, bf16[256,512]{1,0:T(8,128)(2,1)S(1)}, u32[]{:S(2)}, u32[]{:S(2)}) collective-permute-start(bf16[256,512]{1,0:T(8,128)(2,1)S(1)} %pad_maximum_fusion.5), channel_id=1, source_target_pairs={{0,64},{64,0},{128,192},{192,128},{1,65},{65,1},{129,193},{193,129... | collective-permute-start | bytes 786440 | tf_op jit(solution)/shard_map/ppermute | solution.py:46
  75.8 7.0 %collective-permute-start.18 = (bf16[256,512]{1,0:T(8,128)(2,1)S(1)}, bf16[256,512]{1,0:T(8,128)(2,1)S(1)}, u32[]{:S(2)}, u32[]{:S(2)}) collective-permute-start(bf16[256,512]{1,0:T(8,128)(2,1)S(1)} %convolution_convert_fusion.7), channel_id=1, source_target_pairs={{0,57},{1,2},{2,1},{3,4},{4,3},{5,6},{6,5},{7,14},{8,11},{9,16},{1... | collective-permute-start | bytes 786440 | tf_op jit(solution)/shard_map/ppermute | solution.py:42
  84.9 7.4 %collective-permute-start.20 = (bf16[256,512]{1,0:T(8,128)(2,1)}, bf16[256,512]{1,0:T(8,128)(2,1)}, u32[]{:S(2)}, u32[]{:S(2)}) collective-permute-start(bf16[256,512]{1,0:T(8,128)(2,1)} %convolution_convert_fusion.6), channel_id=1, source_target_pairs={{0,57},{1,2},{2,1},{3,4},{4,3},{5,6},{6,5},{7,14},{8,11},{9,16},{1... | collective-permute-start | bytes 786440 | tf_op jit(solution)/shard_map/ppermute | solution.py:42
  94.3 8.9 %collective-permute-start.21 = (bf16[256,512]{1,0:T(8,128)(2,1)S(1)}, bf16[256,512]{1,0:T(8,128)(2,1)S(1)}, u32[]{:S(2)}, u32[]{:S(2)}) collective-permute-start(bf16[256,512]{1,0:T(8,128)(2,1)S(1)} %get-tuple-element.174), channel_id=1, source_target_pairs={{0,192},{64,128},{128,64},{192,0},{1,193},{65,129},{129,65},{193,1... | collective-permute-start | bytes 786440 | tf_op jit(solution)/shard_map/ppermute | solution.py:46
  97.6 13.1 %collective-permute-start.22 = (bf16[256,1024]{1,0:T(8,128)(2,1)S(1)}, bf16[256,1024]{1,0:T(8,128)(2,1)S(1)}, u32[]{:S(2)}, u32[]{:S(2)}) collective-permute-start(bf16[256,1024]{1,0:T(8,128)(2,1)S(1)} %pad_maximum_fusion.1), channel_id=1, source_target_pairs={{0,64},{64,0},{128,192},{192,128},{1,65},{65,1},{129,193},{193,129... | collective-permute-start | bytes 1572872 | tf_op jit(solution)/shard_map/ppermute | solution.py:46
  111.6 2.1 %collective-permute-start.23 = (bf16[256,512]{1,0:T(8,128)(2,1)}, bf16[256,512]{1,0:T(8,128)(2,1)}, u32[]{:S(2)}, u32[]{:S(2)}) collective-permute-start(bf16[256,512]{1,0:T(8,128)(2,1)} %convolution_convert_fusion.5), channel_id=1, source_target_pairs={{0,1},{1,0},{2,3},{3,2},{4,5},{5,4},{6,7},{7,6},{8,9},{9,8},{10,11... | collective-permute-start | bytes 786440 | tf_op jit(solution)/shard_map/ppermute | solution.py:42
  111.6 7.5 %collective-permute-start.24 = (bf16[256,512]{1,0:T(8,128)(2,1)}, bf16[256,512]{1,0:T(8,128)(2,1)S(1)}, u32[]{:S(2)}, u32[]{:S(2)}) collective-permute-start(bf16[256,512]{1,0:T(8,128)(2,1)} %convolution_convert_fusion.5), channel_id=1, source_target_pairs={{0,57},{1,2},{2,1},{3,4},{4,3},{5,6},{6,5},{7,14},{8,11},{9,16},{1... | collective-permute-start | bytes 786440 | tf_op jit(solution)/shard_map/ppermute | solution.py:42
  122.5 7.1 %collective-permute-start.26 = (bf16[256,512]{1,0:T(8,128)(2,1)S(1)}, bf16[256,512]{1,0:T(8,128)(2,1)S(1)}, u32[]{:S(2)}, u32[]{:S(2)}) collective-permute-start(bf16[256,512]{1,0:T(8,128)(2,1)S(1)} %convolution_convert_fusion.4), channel_id=1, source_target_pairs={{0,57},{1,2},{2,1},{3,4},{4,3},{5,6},{6,5},{7,14},{8,11},{9,16},{1... | collective-permute-start | bytes 786440 | tf_op jit(solution)/shard_map/ppermute | solution.py:42
  130.6 7.1 %collective-permute-start.28 = (bf16[256,512]{1,0:T(8,128)(2,1)S(1)}, bf16[256,512]{1,0:T(8,128)(2,1)S(1)}, u32[]{:S(2)}, u32[]{:S(2)}) collective-permute-start(bf16[256,512]{1,0:T(8,128)(2,1)S(1)} %convolution_convert_fusion.3), channel_id=1, source_target_pairs={{0,57},{1,2},{2,1},{3,4},{4,3},{5,6},{6,5},{7,14},{8,11},{9,16},{1... | collective-permute-start | bytes 786440 | tf_op jit(solution)/shard_map/ppermute | solution.py:42
  140.1 7.0 %collective-permute-start.30 = (bf16[256,512]{1,0:T(8,128)(2,1)S(1)}, bf16[256,512]{1,0:T(8,128)(2,1)S(1)}, u32[]{:S(2)}, u32[]{:S(2)}) collective-permute-start(bf16[256,512]{1,0:T(8,128)(2,1)S(1)} %convolution_convert_fusion.2), channel_id=1, source_target_pairs={{0,57},{1,2},{2,1},{3,4},{4,3},{5,6},{6,5},{7,14},{8,11},{9,16},{1... | collective-permute-start | bytes 786440 | tf_op jit(solution)/shard_map/ppermute | solution.py:42
  140.8 7.6 %collective-permute-start.32 = (bf16[128,1536]{1,0:T(8,128)(2,1)S(1)}, bf16[128,1536]{1,0:T(8,128)(2,1)S(1)}, u32[]{:S(2)}, u32[]{:S(2)}) collective-permute-start(bf16[128,1536]{1,0:T(8,128)(2,1)S(1)} %pad_maximum_fusion.2), channel_id=1, source_target_pairs={{0,1},{1,0},{2,3},{3,2},{4,5},{5,4},{6,7},{7,6},{8,9},{9,8},{10,11... | collective-permute-start | bytes 1179656 | tf_op jit(solution)/shard_map/ppermute | solution.py:42
  150.3 9.4 %collective-permute-start.34 = (bf16[32,3072]{1,0:T(8,128)(2,1)S(1)}, bf16[32,3072]{1,0:T(8,128)(2,1)S(1)}, u32[]{:S(2)}, u32[]{:S(2)}) collective-permute-start(bf16[32,3072]{1,0:T(8,128)(2,1)S(1)} %get-tuple-element.144), channel_id=1, source_target_pairs={{0,4},{1,5},{2,6},{3,7},{4,0},{5,1},{6,2},{7,3},{8,12},{9,13},{10,... | collective-permute-start | bytes 589832 | tf_op jit(solution)/shard_map/ppermute | solution.py:42
  150.4 12.5 %collective-permute-start.36 = (bf16[32,3072]{1,0:T(8,128)(2,1)S(1)}, bf16[32,3072]{1,0:T(8,128)(2,1)S(1)}, u32[]{:S(2)}, u32[]{:S(2)}) collective-permute-start(bf16[32,3072]{1,0:T(8,128)(2,1)S(1)} %get-tuple-element.145), channel_id=1, source_target_pairs={{0,6},{1,7},{2,4},{3,5},{4,2},{5,3},{6,0},{7,1},{8,14},{9,15},{10,... | collective-permute-start | bytes 589832 | tf_op jit(solution)/shard_map/ppermute | solution.py:42
  152.3 10.6 %collective-permute-start.35 = (bf16[32,3072]{1,0:T(8,128)(2,1)S(1)}, bf16[32,3072]{1,0:T(8,128)(2,1)S(1)}, u32[]{:S(2)}, u32[]{:S(2)}) collective-permute-start(bf16[32,3072]{1,0:T(8,128)(2,1)S(1)} %get-tuple-element.146), channel_id=1, source_target_pairs={{0,2},{1,3},{2,0},{3,1},{4,6},{5,7},{6,4},{7,5},{8,10},{9,11},{10,... | collective-permute-start | bytes 589832 | tf_op jit(solution)/shard_map/ppermute | solution.py:42
  163.8 14.0 %all-to-all-start = ((bf16[8,4,3072]{2,1,0:T(4,128)(2,1)}), bf16[8,4,3072]{2,1,0:T(4,128)(2,1)S(1)}, u32[]{:S(2)}, u32[]{:S(2)}) async-start(bf16[8,4,3072]{2,1,0:T(4,128)(2,1)} %reshape.255), calls=%async_computation | async-start | bytes 393216 | tf_op jit(solution)/shard_map/all_to_all | solution.py:225
  167.2 14.3 %collective-permute-start.31 = (bf16[256,512]{1,0:T(8,128)(2,1)S(1)}, bf16[256,512]{1,0:T(8,128)(2,1)S(1)}, u32[]{:S(2)}, u32[]{:S(2)}) collective-permute-start(bf16[256,512]{1,0:T(8,128)(2,1)S(1)} %get-tuple-element.150), channel_id=1, source_target_pairs={{0,0},{1,1},{2,2},{3,3},{4,4},{5,5},{6,6},{7,7},{14,8},{15,9},{12,... | collective-permute-start | bytes 786440 | tf_op jit(solution)/shard_map/ppermute | solution.py:42
  177.9 5.4 %collective-permute-start.39 = (bf16[4,3072]{1,0:T(4,128)(2,1)S(1)}, bf16[4,3072]{1,0:T(4,128)(2,1)S(1)}, u32[]{:S(2)}, u32[]{:S(2)}) collective-permute-start(bf16[4,3072]{1,0:T(4,128)(2,1)S(1)} %reduce_sum.12), channel_id=1, source_target_pairs={{0,128},{64,192},{128,0},{192,64},{1,129},{65,193},{129,1},{193,65... | collective-permute-start | bytes 73736 | tf_op jit(solution)/shard_map/ppermute | solution.py:46
  179.2 5.0 %collective-permute-start.38 = (bf16[4,3072]{1,0:T(4,128)(2,1)S(1)}, bf16[4,3072]{1,0:T(4,128)(2,1)S(1)}, u32[]{:S(2)}, u32[]{:S(2)}) collective-permute-start(bf16[4,3072]{1,0:T(4,128)(2,1)S(1)} %reduce_sum.12), channel_id=1, source_target_pairs={{0,192},{64,128},{128,64},{192,0},{1,193},{65,129},{129,65},{193,1... | collective-permute-start | bytes 73736 | tf_op jit(solution)/shard_map/ppermute | solution.py:46
  180.9 3.8 %collective-permute-start.37 = (bf16[4,3072]{1,0:T(4,128)(2,1)S(1)}, bf16[4,3072]{1,0:T(4,128)(2,1)S(1)}, u32[]{:S(2)}, u32[]{:S(2)}) collective-permute-start(bf16[4,3072]{1,0:T(4,128)(2,1)S(1)} %reduce_sum.12), channel_id=1, source_target_pairs={{0,64},{64,0},{128,192},{192,128},{1,65},{65,1},{129,193},{193,129... | collective-permute-start | bytes 73736 | tf_op jit(solution)/shard_map/ppermute | solution.py:46
  (45 other events, 325.5 us)

commit v2 on v0

--- a/solution.py
+++ b/solution.py
@@ -139,7 +139,7 @@
     cot = after(cot, left_hand[3])
     cots = (cot, over_step(cot, 1))
     n_out = over_node(m_out, OUTER)
-    n_chip = jnp.concatenate([m_own, over_node(m_sib, SIBLING)], axis=0)
+    n_all = jnp.concatenate([m_own, over_node(m_sib, SIBLING), n_out], axis=0)
 
     own_first = (x & 1) == 1
 
@@ -208,7 +208,7 @@
                 kept[turn, layer] = after((ab, dzb), dm)
                 keep, sent = split_cores(sum_rows(layer))
                 grads[layer] = keep + over_node(sent, SIBLING).astype(F32)
-            adjoint = adjoint + t_mul(n_chip, jnp.concatenate([dm, d_sib], axis=0)) + t_mul(n_out, d_out)
+            adjoint = adjoint + t_mul(n_all, jnp.concatenate([dm, d_sib, d_out], axis=0))
         result = jnp.where(x == STEPS - 1 - turn, adjoint, result)
     result = over_node(result.astype(BF16), FLIP).astype(F32)
 

time: 165 us -> 176 us (1.067)
  waiting for transfers between devices: 67.3 us -> 76.9 us
  starting transfers between devices: 67.1 us -> 58.6 us
  matrix products: 21.3 us -> 28.7 us
  local copies, waits for them, and re-layouts: 2.19 us -> 4.27 us
    ppermute x31, starting transfers between devices: 53.6 us -> 45.7 us  [over_node(): return lax.ppermute(value, 'node', pairs)]
    dot_general x24, matrix products: 8.98 us -> 14.7 us  [mul_t(): lax.dot_general(left, right, (((1,), (1,)), ((), ())), preferred_element_...]
    ppermute x9, waiting for transfers between devices: 15 us -> 20.4 us  [over_step(): return lax.ppermute(value, 'step', [(s, s ^ k) for s in range(STEPS)])]
    ppermute x31, waiting for transfers between devices: 45.5 us -> 47.9 us  [over_node(): return lax.ppermute(value, 'node', pairs)]
    all_to_all x1, waiting for transfers between devices: 6.85 us -> 8.63 us  [on_device(): lax.all_to_all(sent, 'node', 0, 0, axis_index_groups=Z_GROUPS, tiled=False)]
    dot_general x20 -> x12, matrix products: 7.53 us -> 8.51 us  [t_mul(): lax.dot_general(left, right, (((0,), (0,)), ((), ())), preferred_element_...]
  transfers between devices with their start and end apart: 41 -> 41, of which waited for: 19 -> 26; matrix products, arithmetic and copies ran while one was open for 12% -> 11% of each run, Pallas kernels for 0% -> 0%
where the time goes in v2:
time: 176 us; the launch traced here: 175 us
  waiting for transfers between devices  76.9 us (44%)
  starting transfers between devices  58.6 us (33%)
  matrix products  28.7 us (16%)
  other arithmetic  4.28 us (2%)
  local copies, waits for them, and re-layouts  4.27 us (2%)
  between operations  2.61 us (1%)
    ppermute x31, waiting for transfers between devices, over_node(): return lax.ppermute(value, 'node', pairs)  47.9 us
    ppermute x31, starting transfers between devices, over_node(): return lax.ppermute(value, 'node', pairs)  45.7 us
    ppermute x9, waiting for transfers between devices, over_step(): return lax.ppermute(value, 'step', [(s, s ^ k) for s in range(STEPS)])  20.4 us
    dot_general x24, matrix products, mul_t(): lax.dot_general(left, right, (((1,), (1,)), ((), ())), preferred_element_...  14.7 us
    ppermute x9, starting transfers between devices, over_step(): return lax.ppermute(value, 'step', [(s, s ^ k) for s in range(STEPS)])  9.53 us
    all_to_all x1, waiting for transfers between devices, on_device(): lax.all_to_all(sent, 'node', 0, 0, axis_index_groups=Z_GROUPS, tiled=False)  8.63 us
    dot_general x12, matrix products, t_mul(): lax.dot_general(left, right, (((0,), (0,)), ((), ())), preferred_element_...  8.51 us
    dot_general x12, matrix products, mul(): return jnp.dot(left, right, preferred_element_type=F32)  5.09 us
  transfers between devices with their start and end apart: 41, of which 26 were waited for; matrix products, arithmetic and copies ran while one was open for 11% of the time, Pallas kernels for 0%

profile of v2, /device:TPU:6, one launch (start us, length us, event | category | flops | bytes accessed | tf_op | source)
XLA Modules:
  0.0 175.5 jit_solution(15436258549289231562)
XLA Ops:
  4.5 10.6 %collective-permute-start.4 = (bf16[256,512]{1,0:T(8,128)(2,1)S(1)}, bf16[256,512]{1,0:T(8,128)(2,1)S(1)}, u32[]{:S(2)}, u32[]{:S(2)}) collective-permute-start(bf16[256,512]{1,0:T(8,128)(2,1)S(1)} %bitcast.59), channel_id=1, source_target_pairs={{63,0},{2,1},{1,2},{4,3},{3,4},{6,5},{5,6},{8,7},{13,8},{16,9},{11... | collective-permute-start | bytes 786440 | tf_op jit(solution)/shard_map/ppermute | solution.py:42
  16.3 5.2 %collective-permute-done.4 = bf16[256,512]{1,0:T(8,128)(2,1)S(1)} collective-permute-done((bf16[256,512]{1,0:T(8,128)(2,1)S(1)}, bf16[256,512]{1,0:T(8,128)(2,1)S(1)}, u32[]{:S(2)}, u32[]{:S(2)}) %collective-permute-start.4) | collective-permute-done | bytes 262176 | tf_op jit(solution)/shard_map/ppermute | solution.py:42
  23.9 12.4 %collective-permute-start.7 = (bf16[256,512]{1,0:T(8,128)(2,1)S(1)}, bf16[256,512]{1,0:T(8,128)(2,1)S(1)}, u32[]{:S(2)}, u32[]{:S(2)}) collective-permute-start(bf16[256,512]{1,0:T(8,128)(2,1)S(1)} %convert_add_fusion.3), channel_id=1, source_target_pairs={{0,57},{1,2},{2,1},{3,4},{4,3},{5,6},{6,5},{7,14},{8,11},{9,16},{1... | collective-permute-start | bytes 786440 | tf_op jit(solution)/shard_map/ppermute | solution.py:42
  37.4 3.0 %collective-permute-done.7 = bf16[256,512]{1,0:T(8,128)(2,1)S(1)} collective-permute-done((bf16[256,512]{1,0:T(8,128)(2,1)S(1)}, bf16[256,512]{1,0:T(8,128)(2,1)S(1)}, u32[]{:S(2)}, u32[]{:S(2)}) %collective-permute-start.7) | collective-permute-done | bytes 262176 | tf_op jit(solution)/shard_map/ppermute | solution.py:42
  43.3 5.5 %collective-permute-done.8 = bf16[256,512]{1,0:T(8,128)(2,1)S(1)} collective-permute-done((bf16[256,512]{1,0:T(8,128)(2,1)S(1)}, bf16[256,512]{1,0:T(8,128)(2,1)S(1)}, u32[]{:S(2)}, u32[]{:S(2)}) %collective-permute-start.8) | collective-permute-done | bytes 262176 | tf_op jit(solution)/shard_map/ppermute | solution.py:46
  51.7 2.3 %convolution_add_fusion.17 = f32[256,512]{1,0:T(8,128)} fusion(bf16[256,512]{1,0:T(8,128)(2,1)S(1)} %fusion.4, bf16[256,512]{1,0:T(8,128)(2,1)S(1)} %get-tuple-element.114, bf16[512,3072]{1,0:T(8,128)(2,1)} %param.9), kind=kOutput, calls=%fused_computation.33 | convolution fusion | flops 134479872 | bytes 1572864 | tf_op jit(solution)/shard_map/dot_general | solution.py:63
  54.0 4.0 %collective-permute-start.12 = (bf16[256,512]{1,0:T(8,128)(2,1)S(1)}, bf16[256,512]{1,0:T(8,128)(2,1)}, u32[]{:S(2)}, u32[]{:S(2)}) collective-permute-start(bf16[256,512]{1,0:T(8,128)(2,1)S(1)} %convolution_convert_fusion.9), channel_id=1, source_target_pairs={{0,57},{1,2},{2,1},{3,4},{4,3},{5,6},{6,5},{7,14},{8,11},{9,16},{1... | collective-permute-start | bytes 786440 | tf_op jit(solution)/shard_map/ppermute | solution.py:42
  59.6 4.1 %collective-permute-done.10 = bf16[256,256]{0,1:T(8,128)(2,1)S(1)} collective-permute-done((bf16[256,256]{0,1:T(8,128)(2,1)S(1)}, bf16[256,256]{0,1:T(8,128)(2,1)S(1)}, u32[]{:S(2)}, u32[]{:S(2)}) %collective-permute-start.10) | collective-permute-done | bytes 131104 | tf_op jit(solution)/shard_map/ppermute | solution.py:42
  63.8 1.8 %convolution_add_fusion.7 = f32[256,512]{1,0:T(8,128)S(1)} fusion(f32[256,512]{1,0:T(8,128)} %convolution_add_fusion.17, bf16[256,512]{1,0:T(8,128)(2,1)} %collective-permute-done.12, bf16[256,512]{1,0:T(8,128)(2,1)} %collective-permute-done.11, bf16[256,512]{1,0:T(8,128)(2,1)} %copy-done.34, bf16[256,256]{0,1:T(8,128)(2,1)S(1)} %collective-permute-done.10, ...), kind=kOutput, calls=%fused_computation.13 | convolution fusion | flops 204996608 | bytes 2228224 | tf_op jit(solution)/shard_map/dot_general | solution.py:67
  65.6 1.5 collective-permute-done.13
  68.2 1.8 %collective-permute-start.15 = (bf16[256,512]{1,0:T(8,128)(2,1)S(1)}, bf16[256,512]{1,0:T(8,128)(2,1)S(1)}, u32[]{:S(2)}, u32[]{:S(2)}) collective-permute-start(bf16[256,512]{1,0:T(8,128)(2,1)S(1)} %convolution_convert_fusion.8), channel_id=1, source_target_pairs={{0,57},{1,2},{2,1},{3,4},{4,3},{5,6},{6,5},{7,14},{8,11},{9,16},{1... | collective-permute-start | bytes 786440 | tf_op jit(solution)/shard_map/ppermute | solution.py:42
  71.5 3.8 %collective-permute-done.15 = bf16[256,512]{1,0:T(8,128)(2,1)S(1)} collective-permute-done((bf16[256,512]{1,0:T(8,128)(2,1)S(1)}, bf16[256,512]{1,0:T(8,128)(2,1)S(1)}, u32[]{:S(2)}, u32[]{:S(2)}) %collective-permute-start.15) | collective-permute-done | bytes 262176 | tf_op jit(solution)/shard_map/ppermute | solution.py:42
  76.8 1.8 %collective-permute-start.17 = (bf16[256,512]{1,0:T(8,128)(2,1)S(1)}, bf16[256,512]{1,0:T(8,128)(2,1)S(1)}, u32[]{:S(2)}, u32[]{:S(2)}) collective-permute-start(bf16[256,512]{1,0:T(8,128)(2,1)S(1)} %convolution_convert_fusion.7), channel_id=1, source_target_pairs={{0,57},{1,2},{2,1},{3,4},{4,3},{5,6},{6,5},{7,14},{8,11},{9,16},{1... | collective-permute-start | bytes 786440 | tf_op jit(solution)/shard_map/ppermute | solution.py:42
  80.1 3.8 %collective-permute-done.17 = bf16[256,512]{1,0:T(8,128)(2,1)S(1)} collective-permute-done((bf16[256,512]{1,0:T(8,128)(2,1)S(1)}, bf16[256,512]{1,0:T(8,128)(2,1)S(1)}, u32[]{:S(2)}, u32[]{:S(2)}) %collective-permute-start.17) | collective-permute-done | bytes 262176 | tf_op jit(solution)/shard_map/ppermute | solution.py:42
  85.3 1.8 %collective-permute-start.19 = (bf16[256,512]{1,0:T(8,128)(2,1)S(1)}, bf16[256,512]{1,0:T(8,128)(2,1)S(1)}, u32[]{:S(2)}, u32[]{:S(2)}) collective-permute-start(bf16[256,512]{1,0:T(8,128)(2,1)S(1)} %convolution_convert_fusion.6), channel_id=1, source_target_pairs={{0,57},{1,2},{2,1},{3,4},{4,3},{5,6},{6,5},{7,14},{8,11},{9,16},{1... | collective-permute-start | bytes 786440 | tf_op jit(solution)/shard_map/ppermute | solution.py:42
  88.6 3.8 %collective-permute-done.19 = bf16[256,512]{1,0:T(8,128)(2,1)S(1)} collective-permute-done((bf16[256,512]{1,0:T(8,128)(2,1)S(1)}, bf16[256,512]{1,0:T(8,128)(2,1)S(1)}, u32[]{:S(2)}, u32[]{:S(2)}) %collective-permute-start.19) | collective-permute-done | bytes 262176 | tf_op jit(solution)/shard_map/ppermute | solution.py:42
  94.4 6.0 %collective-permute-done.20 = bf16[256,512]{1,0:T(8,128)(2,1)S(1)} collective-permute-done((bf16[256,512]{1,0:T(8,128)(2,1)S(1)}, bf16[256,512]{1,0:T(8,128)(2,1)S(1)}, u32[]{:S(2)}, u32[]{:S(2)}) %collective-permute-start.20) | collective-permute-done | bytes 262176 | tf_op jit(solution)/shard_map/ppermute | solution.py:46
  105.4 2.1 %collective-permute-start.23 = (bf16[256,512]{1,0:T(8,128)(2,1)}, bf16[256,512]{1,0:T(8,128)(2,1)}, u32[]{:S(2)}, u32[]{:S(2)}) collective-permute-start(bf16[256,512]{1,0:T(8,128)(2,1)} %convolution_convert_fusion.5), channel_id=1, source_target_pairs={{0,57},{1,2},{2,1},{3,4},{4,3},{5,6},{6,5},{7,14},{8,11},{9,16},{1... | collective-permute-start | bytes 786440 | tf_op jit(solution)/shard_map/ppermute | solution.py:42
  108.6 4.1 %collective-permute-done.23 = bf16[256,512]{1,0:T(8,128)(2,1)} collective-permute-done((bf16[256,512]{1,0:T(8,128)(2,1)}, bf16[256,512]{1,0:T(8,128)(2,1)}, u32[]{:S(2)}, u32[]{:S(2)}) %collective-permute-start.23) | collective-permute-done | bytes 262176 | tf_op jit(solution)/shard_map/ppermute | solution.py:42
  112.7 1.8 %broadcast_select_fusion.5 = (bf16[256,512]{1,0:T(8,128)(2,1)S(1)}, f32[256,512]{1,0:T(8,128)S(1)}) fusion(pred[]{:T(512)S(6)} %ge.3, f32[256,512]{1,0:T(8,128)S(1)} %convolution_add_fusion.7, f32[256,512]{1,0:T(8,128)} %convolution_add_fusion.13, bf16[256,512]{1,0:T(8,128)(2,1)} %collective-permute-done.23, bf16[256,512]{1,0:T(8,128)(2,1)} %collective-permute-done.22, ...), kind=kOutput, calls=%fused_computation.201 | convolution fusion | flops 205389824 | bytes 3014657 | tf_op jit(solution)/shard_map/dot_general | solution.py:67
  115.7 2.2 %collective-permute-start.25 = (bf16[256,512]{1,0:T(8,128)(2,1)S(1)}, bf16[256,512]{1,0:T(8,128)(2,1)S(1)}, u32[]{:S(2)}, u32[]{:S(2)}) collective-permute-start(bf16[256,512]{1,0:T(8,128)(2,1)S(1)} %convolution_convert_fusion.4), channel_id=1, source_target_pairs={{0,57},{1,2},{2,1},{3,4},{4,3},{5,6},{6,5},{7,14},{8,11},{9,16},{1... | collective-permute-start | bytes 786440 | tf_op jit(solution)/shard_map/ppermute | solution.py:42
  119.5 3.4 %collective-permute-done.25 = bf16[256,512]{1,0:T(8,128)(2,1)S(1)} collective-permute-done((bf16[256,512]{1,0:T(8,128)(2,1)S(1)}, bf16[256,512]{1,0:T(8,128)(2,1)S(1)}, u32[]{:S(2)}, u32[]{:S(2)}) %collective-permute-start.25) | collective-permute-done | bytes 262176 | tf_op jit(solution)/shard_map/ppermute | solution.py:42
  123.9 3.2 %collective-permute-done.26 = bf16[256,512]{1,0:T(8,128)(2,1)S(1)} collective-permute-done((bf16[256,512]{1,0:T(8,128)(2,1)S(1)}, bf16[256,512]{1,0:T(8,128)(2,1)S(1)}, u32[]{:S(2)}, u32[]{:S(2)}) %collective-permute-start.26) | collective-permute-done | bytes 262176 | tf_op jit(solution)/shard_map/ppermute | solution.py:46
  130.4 3.9 %collective-permute-done.28 = bf16[256,512]{1,0:T(8,128)(2,1)S(1)} collective-permute-done((bf16[256,512]{1,0:T(8,128)(2,1)S(1)}, bf16[256,512]{1,0:T(8,128)(2,1)S(1)}, u32[]{:S(2)}, u32[]{:S(2)}) %collective-permute-start.28) | collective-permute-done | bytes 262176 | tf_op jit(solution)/shard_map/ppermute | solution.py:42
  139.6 3.0 %collective-permute-start.36 = (bf16[32,3072]{1,0:T(8,128)(2,1)S(1)}, bf16[32,3072]{1,0:T(8,128)(2,1)S(1)}, u32[]{:S(2)}, u32[]{:S(2)}) collective-permute-start(bf16[32,3072]{1,0:T(8,128)(2,1)S(1)} %get-tuple-element.101), channel_id=1, source_target_pairs={{0,6},{1,7},{2,4},{3,5},{4,2},{5,3},{6,0},{7,1},{8,14},{9,15},{10,... | collective-permute-start | bytes 589832 | tf_op jit(solution)/shard_map/ppermute | solution.py:42
  143.0 4.7 %collective-permute-done.34 = bf16[32,3072]{1,0:T(8,128)(2,1)S(1)} collective-permute-done((bf16[32,3072]{1,0:T(8,128)(2,1)S(1)}, bf16[32,3072]{1,0:T(8,128)(2,1)S(1)}, u32[]{:S(2)}, u32[]{:S(2)}) %collective-permute-start.34) | collective-permute-done | bytes 196640 | tf_op jit(solution)/shard_map/ppermute | solution.py:42
  147.7 2.0 %collective-permute-done.35 = bf16[32,3072]{1,0:T(8,128)(2,1)S(1)} collective-permute-done((bf16[32,3072]{1,0:T(8,128)(2,1)S(1)}, bf16[32,3072]{1,0:T(8,128)(2,1)S(1)}, u32[]{:S(2)}, u32[]{:S(2)}) %collective-permute-start.35) | collective-permute-done | bytes 196640 | tf_op jit(solution)/shard_map/ppermute | solution.py:42
  152.0 3.4 %all-to-all-start = ((bf16[8,4,3072]{2,1,0:T(4,128)(2,1)}), bf16[8,4,3072]{2,1,0:T(4,128)(2,1)S(1)}, u32[]{:S(2)}, u32[]{:S(2)}) async-start(bf16[8,4,3072]{2,1,0:T(4,128)(2,1)} %reshape.255), calls=%async_computation | async-start | bytes 393216 | tf_op jit(solution)/shard_map/all_to_all | solution.py:222
  155.4 1.5 fusion.14
  157.6 8.6 %all-to-all-done = bf16[8,4,3072]{2,1,0:T(4,128)(2,1)S(1)} async-done(((bf16[8,4,3072]{2,1,0:T(4,128)(2,1)}), bf16[8,4,3072]{2,1,0:T(4,128)(2,1)S(1)}, u32[]{:S(2)}, u32[]{:S(2)}) %all-to-all-start) | async-done | bytes 196640 | tf_op jit(solution)/shard_map/all_to_all | solution.py:222
  167.3 2.2 %collective-permute-start.38 = (bf16[4,3072]{1,0:T(4,128)(2,1)S(1)}, bf16[4,3072]{1,0:T(4,128)(2,1)S(1)}, u32[]{:S(2)}, u32[]{:S(2)}) collective-permute-start(bf16[4,3072]{1,0:T(4,128)(2,1)S(1)} %reduce_sum.12), channel_id=1, source_target_pairs={{0,192},{64,128},{128,64},{192,0},{1,193},{65,129},{129,65},{193,1... | collective-permute-start | bytes 73736 | tf_op jit(solution)/shard_map/ppermute | solution.py:46
  172.4 2.4 %collective-permute-done.39 = bf16[4,3072]{1,0:T(4,128)(2,1)S(1)} collective-permute-done((bf16[4,3072]{1,0:T(4,128)(2,1)S(1)}, bf16[4,3072]{1,0:T(4,128)(2,1)S(1)}, u32[]{:S(2)}, u32[]{:S(2)}) %collective-permute-start.39) | collective-permute-done | bytes 24608 | tf_op jit(solution)/shard_map/ppermute | solution.py:46
  (231 shorter events, 51.4 us)
Async XLA Ops:
  3.1 12.9 %collective-permute-start.2 = (bf16[256,768]{0,1:T(8,128)(2,1)S(1)}, bf16[256,768]{0,1:T(8,128)(2,1)S(1)}, u32[]{:S(2)}, u32[]{:S(2)}) collective-permute-start(bf16[256,768]{0,1:T(8,128)(2,1)S(1)} %bitcast.57), channel_id=1, source_target_pairs={{0,0},{1,1},{2,2},{3,3},{4,4},{5,5},{6,6},{7,7},{14,8},{15,9},{12,... | collective-permute-start | bytes 1179656 | tf_op jit(solution)/shard_map/ppermute | solution.py:42
  3.8 12.1 %collective-permute-start.1 = (bf16[256,512]{1,0:T(8,128)(2,1)S(1)}, bf16[256,512]{1,0:T(8,128)(2,1)S(1)}, u32[]{:S(2)}, u32[]{:S(2)}) collective-permute-start(bf16[256,512]{1,0:T(8,128)(2,1)S(1)} %bitcast.58), channel_id=1, source_target_pairs={{0,0},{1,1},{2,2},{3,3},{4,4},{5,5},{6,6},{7,7},{14,8},{15,9},{12,... | collective-permute-start | bytes 786440 | tf_op jit(solution)/shard_map/ppermute | solution.py:42
  4.5 17.0 %collective-permute-start.4 = (bf16[256,512]{1,0:T(8,128)(2,1)S(1)}, bf16[256,512]{1,0:T(8,128)(2,1)S(1)}, u32[]{:S(2)}, u32[]{:S(2)}) collective-permute-start(bf16[256,512]{1,0:T(8,128)(2,1)S(1)} %bitcast.59), channel_id=1, source_target_pairs={{63,0},{2,1},{1,2},{4,3},{3,4},{6,5},{5,6},{8,7},{13,8},{16,9},{11... | collective-permute-start | bytes 786440 | tf_op jit(solution)/shard_map/ppermute | solution.py:42
  15.1 21.2 %collective-permute-start = (bf16[256,512]{1,0:T(8,128)(2,1)S(1)}, bf16[256,512]{1,0:T(8,128)(2,1)S(1)}, u32[]{:S(2)}, u32[]{:S(2)}) collective-permute-start(bf16[256,512]{1,0:T(8,128)(2,1)S(1)} %convert_element_type.177), channel_id=1, source_target_pairs={{0,0},{1,1},{2,2},{3,3},{4,4},{5,5},{6,6},{7,7},{14,8},{15,9},{12,... | collective-permute-start | bytes 786440 | tf_op jit(solution)/shard_map/ppermute | solution.py:42
  15.9 5.8 %collective-permute-start.3 = (bf16[256,512]{1,0:T(8,128)(2,1)S(1)}, bf16[256,512]{1,0:T(8,128)(2,1)S(1)}, u32[]{:S(2)}, u32[]{:S(2)}) collective-permute-start(bf16[256,512]{1,0:T(8,128)(2,1)S(1)} %collective-permute-done.1), channel_id=1, source_target_pairs={{0,1},{1,0},{2,3},{3,2},{4,5},{5,4},{6,7},{7,6},{8,9},{9,8},{10,11... | collective-permute-start | bytes 786440 | tf_op jit(solution)/shard_map/ppermute | solution.py:42
  23.8 13.3 %collective-permute-start.6 = (bf16[256,512]{1,0:T(8,128)(2,1)S(1)}, bf16[256,512]{1,0:T(8,128)(2,1)S(1)}, u32[]{:S(2)}, u32[]{:S(2)}) collective-permute-start(bf16[256,512]{1,0:T(8,128)(2,1)S(1)} %convert_add_fusion.3), channel_id=1, source_target_pairs={{0,1},{1,0},{2,3},{3,2},{4,5},{5,4},{6,7},{7,6},{8,9},{9,8},{10,11... | collective-permute-start | bytes 786440 | tf_op jit(solution)/shard_map/ppermute | solution.py:42
  23.9 16.4 %collective-permute-start.7 = (bf16[256,512]{1,0:T(8,128)(2,1)S(1)}, bf16[256,512]{1,0:T(8,128)(2,1)S(1)}, u32[]{:S(2)}, u32[]{:S(2)}) collective-permute-start(bf16[256,512]{1,0:T(8,128)(2,1)S(1)} %convert_add_fusion.3), channel_id=1, source_target_pairs={{0,57},{1,2},{2,1},{3,4},{4,3},{5,6},{6,5},{7,14},{8,11},{9,16},{1... | collective-permute-start | bytes 786440 | tf_op jit(solution)/shard_map/ppermute | solution.py:42
  36.3 6.9 %collective-permute-start.5 = (bf16[256,512]{1,0:T(8,128)(2,1)S(1)}, bf16[256,512]{1,0:T(8,128)(2,1)S(1)}, u32[]{:S(2)}, u32[]{:S(2)}) collective-permute-start(bf16[256,512]{1,0:T(8,128)(2,1)S(1)} %collective-permute-done), channel_id=1, source_target_pairs={{0,64},{64,0},{128,192},{192,128},{1,65},{65,1},{129,193},{193,129... | collective-permute-start | bytes 786440 | tf_op jit(solution)/shard_map/ppermute | solution.py:46
  42.4 6.4 %collective-permute-start.8 = (bf16[256,512]{1,0:T(8,128)(2,1)S(1)}, bf16[256,512]{1,0:T(8,128)(2,1)S(1)}, u32[]{:S(2)}, u32[]{:S(2)}) collective-permute-start(bf16[256,512]{1,0:T(8,128)(2,1)S(1)} %get-tuple-element.112), channel_id=1, source_target_pairs={{0,64},{64,0},{128,192},{192,128},{1,65},{65,1},{129,193},{193,129... | collective-permute-start | bytes 786440 | tf_op jit(solution)/shard_map/ppermute | solution.py:46
  54.0 9.8 %collective-permute-start.12 = (bf16[256,512]{1,0:T(8,128)(2,1)S(1)}, bf16[256,512]{1,0:T(8,128)(2,1)}, u32[]{:S(2)}, u32[]{:S(2)}) collective-permute-start(bf16[256,512]{1,0:T(8,128)(2,1)S(1)} %convolution_convert_fusion.9), channel_id=1, source_target_pairs={{0,57},{1,2},{2,1},{3,4},{4,3},{5,6},{6,5},{7,14},{8,11},{9,16},{1... | collective-permute-start | bytes 786440 | tf_op jit(solution)/shard_map/ppermute | solution.py:42
  58.0 5.8 %collective-permute-start.11 = (bf16[256,512]{1,0:T(8,128)(2,1)S(1)}, bf16[256,512]{1,0:T(8,128)(2,1)}, u32[]{:S(2)}, u32[]{:S(2)}) collective-permute-start(bf16[256,512]{1,0:T(8,128)(2,1)S(1)} %convolution_convert_fusion.9), channel_id=1, source_target_pairs={{0,1},{1,0},{2,3},{3,2},{4,5},{5,4},{6,7},{7,6},{8,9},{9,8},{10,11... | collective-permute-start | bytes 786440 | tf_op jit(solution)/shard_map/ppermute | solution.py:42
  58.1 5.7 %collective-permute-start.10 = (bf16[256,256]{0,1:T(8,128)(2,1)S(1)}, bf16[256,256]{0,1:T(8,128)(2,1)S(1)}, u32[]{:S(2)}, u32[]{:S(2)}) collective-permute-start(bf16[256,256]{0,1:T(8,128)(2,1)S(1)} %get-tuple-element.118), channel_id=1, source_target_pairs={{0,57},{1,2},{2,1},{3,4},{4,3},{5,6},{6,5},{7,14},{8,11},{9,16},{1... | collective-permute-start | bytes 393224 | tf_op jit(solution)/shard_map/ppermute | solution.py:42
  58.3 5.4 %collective-permute-start.9 = (bf16[256,256]{0,1:T(8,128)(2,1)S(1)}, bf16[256,256]{0,1:T(8,128)(2,1)S(1)}, u32[]{:S(2)}, u32[]{:S(2)}) collective-permute-start(bf16[256,256]{0,1:T(8,128)(2,1)S(1)} %get-tuple-element.119), channel_id=1, source_target_pairs={{0,1},{1,0},{2,3},{3,2},{4,5},{5,4},{6,7},{7,6},{8,9},{9,8},{10,11... | collective-permute-start | bytes 393224 | tf_op jit(solution)/shard_map/ppermute | solution.py:42
  58.8 8.3 %collective-permute-start.13 = (bf16[256,512]{1,0:T(8,128)(2,1)S(1)}, bf16[256,512]{1,0:T(8,128)(2,1)S(1)}, u32[]{:S(2)}, u32[]{:S(2)}) collective-permute-start(bf16[256,512]{1,0:T(8,128)(2,1)S(1)} %get-tuple-element.39), channel_id=1, source_target_pairs={{0,64},{64,0},{128,192},{192,128},{1,65},{65,1},{129,193},{193,129... | collective-permute-start | bytes 786440 | tf_op jit(solution)/shard_map/ppermute | solution.py:46
  68.2 7.1 %collective-permute-start.15 = (bf16[256,512]{1,0:T(8,128)(2,1)S(1)}, bf16[256,512]{1,0:T(8,128)(2,1)S(1)}, u32[]{:S(2)}, u32[]{:S(2)}) collective-permute-start(bf16[256,512]{1,0:T(8,128)(2,1)S(1)} %convolution_convert_fusion.8), channel_id=1, source_target_pairs={{0,57},{1,2},{2,1},{3,4},{4,3},{5,6},{6,5},{7,14},{8,11},{9,16},{1... | collective-permute-start | bytes 786440 | tf_op jit(solution)/shard_map/ppermute | solution.py:42
  76.8 7.1 %collective-permute-start.17 = (bf16[256,512]{1,0:T(8,128)(2,1)S(1)}, bf16[256,512]{1,0:T(8,128)(2,1)S(1)}, u32[]{:S(2)}, u32[]{:S(2)}) collective-permute-start(bf16[256,512]{1,0:T(8,128)(2,1)S(1)} %convolution_convert_fusion.7), channel_id=1, source_target_pairs={{0,57},{1,2},{2,1},{3,4},{4,3},{5,6},{6,5},{7,14},{8,11},{9,16},{1... | collective-permute-start | bytes 786440 | tf_op jit(solution)/shard_map/ppermute | solution.py:42
  85.3 7.1 %collective-permute-start.19 = (bf16[256,512]{1,0:T(8,128)(2,1)S(1)}, bf16[256,512]{1,0:T(8,128)(2,1)S(1)}, u32[]{:S(2)}, u32[]{:S(2)}) collective-permute-start(bf16[256,512]{1,0:T(8,128)(2,1)S(1)} %convolution_convert_fusion.6), channel_id=1, source_target_pairs={{0,57},{1,2},{2,1},{3,4},{4,3},{5,6},{6,5},{7,14},{8,11},{9,16},{1... | collective-permute-start | bytes 786440 | tf_op jit(solution)/shard_map/ppermute | solution.py:42
  92.8 7.7 %collective-permute-start.20 = (bf16[256,512]{1,0:T(8,128)(2,1)S(1)}, bf16[256,512]{1,0:T(8,128)(2,1)S(1)}, u32[]{:S(2)}, u32[]{:S(2)}) collective-permute-start(bf16[256,512]{1,0:T(8,128)(2,1)S(1)} %convolution_add_fusion.4), channel_id=1, source_target_pairs={{0,192},{64,128},{128,64},{192,0},{1,193},{65,129},{129,65},{193,1... | collective-permute-start | bytes 786440 | tf_op jit(solution)/shard_map/ppermute | solution.py:46
  93.5 11.2 %collective-permute-start.21 = (bf16[256,1024]{1,0:T(8,128)(2,1)S(1)}, bf16[256,1024]{1,0:T(8,128)(2,1)S(1)}, u32[]{:S(2)}, u32[]{:S(2)}) collective-permute-start(bf16[256,1024]{1,0:T(8,128)(2,1)S(1)} %pad_maximum_fusion.1), channel_id=1, source_target_pairs={{0,64},{64,0},{128,192},{192,128},{1,65},{65,1},{129,193},{193,129... | collective-permute-start | bytes 1572872 | tf_op jit(solution)/shard_map/ppermute | solution.py:46
  105.4 7.3 %collective-permute-start.23 = (bf16[256,512]{1,0:T(8,128)(2,1)}, bf16[256,512]{1,0:T(8,128)(2,1)}, u32[]{:S(2)}, u32[]{:S(2)}) collective-permute-start(bf16[256,512]{1,0:T(8,128)(2,1)} %convolution_convert_fusion.5), channel_id=1, source_target_pairs={{0,57},{1,2},{2,1},{3,4},{4,3},{5,6},{6,5},{7,14},{8,11},{9,16},{1... | collective-permute-start | bytes 786440 | tf_op jit(solution)/shard_map/ppermute | solution.py:42
  115.7 7.1 %collective-permute-start.25 = (bf16[256,512]{1,0:T(8,128)(2,1)S(1)}, bf16[256,512]{1,0:T(8,128)(2,1)S(1)}, u32[]{:S(2)}, u32[]{:S(2)}) collective-permute-start(bf16[256,512]{1,0:T(8,128)(2,1)S(1)} %convolution_convert_fusion.4), channel_id=1, source_target_pairs={{0,57},{1,2},{2,1},{3,4},{4,3},{5,6},{6,5},{7,14},{8,11},{9,16},{1... | collective-permute-start | bytes 786440 | tf_op jit(solution)/shard_map/ppermute | solution.py:42
  118.1 9.0 %collective-permute-start.26 = (bf16[256,512]{1,0:T(8,128)(2,1)S(1)}, bf16[256,512]{1,0:T(8,128)(2,1)S(1)}, u32[]{:S(2)}, u32[]{:S(2)}) collective-permute-start(bf16[256,512]{1,0:T(8,128)(2,1)S(1)} %pad_maximum_fusion.5), channel_id=1, source_target_pairs={{0,64},{64,0},{128,192},{192,128},{1,65},{65,1},{129,193},{193,129... | collective-permute-start | bytes 786440 | tf_op jit(solution)/shard_map/ppermute | solution.py:46
  127.2 7.1 %collective-permute-start.28 = (bf16[256,512]{1,0:T(8,128)(2,1)S(1)}, bf16[256,512]{1,0:T(8,128)(2,1)S(1)}, u32[]{:S(2)}, u32[]{:S(2)}) collective-permute-start(bf16[256,512]{1,0:T(8,128)(2,1)S(1)} %convolution_convert_fusion.3), channel_id=1, source_target_pairs={{0,57},{1,2},{2,1},{3,4},{4,3},{5,6},{6,5},{7,14},{8,11},{9,16},{1... | collective-permute-start | bytes 786440 | tf_op jit(solution)/shard_map/ppermute | solution.py:42
  129.1 7.8 %collective-permute-start.33 = (bf16[128,1536]{1,0:T(8,128)(2,1)S(1)}, bf16[128,1536]{1,0:T(8,128)(2,1)S(1)}, u32[]{:S(2)}, u32[]{:S(2)}) collective-permute-start(bf16[128,1536]{1,0:T(8,128)(2,1)S(1)} %pad_maximum_fusion.4), channel_id=1, source_target_pairs={{0,1},{1,0},{2,3},{3,2},{4,5},{5,4},{6,7},{7,6},{8,9},{9,8},{10,11... | collective-permute-start | bytes 1179656 | tf_op jit(solution)/shard_map/ppermute | solution.py:42
  136.8 18.6 %collective-permute-start.30 = (bf16[256,512]{1,0:T(8,128)(2,1)S(1)}, bf16[256,512]{1,0:T(8,128)(2,1)}, u32[]{:S(2)}, u32[]{:S(2)}) collective-permute-start(bf16[256,512]{1,0:T(8,128)(2,1)S(1)} %convolution_convert_fusion.2), channel_id=1, source_target_pairs={{0,57},{1,2},{2,1},{3,4},{4,3},{5,6},{6,5},{7,14},{8,11},{9,16},{1... | collective-permute-start | bytes 786440 | tf_op jit(solution)/shard_map/ppermute | solution.py:42
  138.4 9.4 %collective-permute-start.34 = (bf16[32,3072]{1,0:T(8,128)(2,1)S(1)}, bf16[32,3072]{1,0:T(8,128)(2,1)S(1)}, u32[]{:S(2)}, u32[]{:S(2)}) collective-permute-start(bf16[32,3072]{1,0:T(8,128)(2,1)S(1)} %get-tuple-element.100), channel_id=1, source_target_pairs={{0,4},{1,5},{2,6},{3,7},{4,0},{5,1},{6,2},{7,3},{8,12},{9,13},{10,... | collective-permute-start | bytes 589832 | tf_op jit(solution)/shard_map/ppermute | solution.py:42
  138.5 11.2 %collective-permute-start.35 = (bf16[32,3072]{1,0:T(8,128)(2,1)S(1)}, bf16[32,3072]{1,0:T(8,128)(2,1)S(1)}, u32[]{:S(2)}, u32[]{:S(2)}) collective-permute-start(bf16[32,3072]{1,0:T(8,128)(2,1)S(1)} %get-tuple-element.102), channel_id=1, source_target_pairs={{0,2},{1,3},{2,0},{3,1},{4,6},{5,7},{6,4},{7,5},{8,10},{9,11},{10,... | collective-permute-start | bytes 589832 | tf_op jit(solution)/shard_map/ppermute | solution.py:42
  139.6 11.5 %collective-permute-start.36 = (bf16[32,3072]{1,0:T(8,128)(2,1)S(1)}, bf16[32,3072]{1,0:T(8,128)(2,1)S(1)}, u32[]{:S(2)}, u32[]{:S(2)}) collective-permute-start(bf16[32,3072]{1,0:T(8,128)(2,1)S(1)} %get-tuple-element.101), channel_id=1, source_target_pairs={{0,6},{1,7},{2,4},{3,5},{4,2},{5,3},{6,0},{7,1},{8,14},{9,15},{10,... | collective-permute-start | bytes 589832 | tf_op jit(solution)/shard_map/ppermute | solution.py:42
  142.9 12.4 %collective-permute-start.29 = (bf16[256,512]{1,0:T(8,128)(2,1)S(1)}, bf16[256,512]{1,0:T(8,128)(2,1)}, u32[]{:S(2)}, u32[]{:S(2)}) collective-permute-start(bf16[256,512]{1,0:T(8,128)(2,1)S(1)} %convolution_convert_fusion.2), channel_id=1, source_target_pairs={{0,1},{1,0},{2,3},{3,2},{4,5},{5,4},{6,7},{7,6},{8,9},{9,8},{10,11... | collective-permute-start | bytes 786440 | tf_op jit(solution)/shard_map/ppermute | solution.py:42
  152.0 14.2 %all-to-all-start = ((bf16[8,4,3072]{2,1,0:T(4,128)(2,1)}), bf16[8,4,3072]{2,1,0:T(4,128)(2,1)S(1)}, u32[]{:S(2)}, u32[]{:S(2)}) async-start(bf16[8,4,3072]{2,1,0:T(4,128)(2,1)} %reshape.255), calls=%async_computation | async-start | bytes 393216 | tf_op jit(solution)/shard_map/all_to_all | solution.py:222
  156.9 13.7 %collective-permute-start.31 = (bf16[256,512]{1,0:T(8,128)(2,1)S(1)}, bf16[256,512]{1,0:T(8,128)(2,1)S(1)}, u32[]{:S(2)}, u32[]{:S(2)}) collective-permute-start(bf16[256,512]{1,0:T(8,128)(2,1)S(1)} %fusion.14), channel_id=1, source_target_pairs={{0,0},{1,1},{2,2},{3,3},{4,4},{5,5},{6,6},{7,7},{14,8},{15,9},{12,... | collective-permute-start | bytes 786440 | tf_op jit(solution)/shard_map/ppermute | solution.py:42
  169.4 5.3 %collective-permute-start.39 = (bf16[4,3072]{1,0:T(4,128)(2,1)S(1)}, bf16[4,3072]{1,0:T(4,128)(2,1)S(1)}, u32[]{:S(2)}, u32[]{:S(2)}) collective-permute-start(bf16[4,3072]{1,0:T(4,128)(2,1)S(1)} %reduce_sum.12), channel_id=1, source_target_pairs={{0,128},{64,192},{128,0},{192,64},{1,129},{65,193},{129,1},{193,65... | collective-permute-start | bytes 73736 | tf_op jit(solution)/shard_map/ppermute | solution.py:46
  (54 other events, 297.9 us)
